TPU v7x, 256 devices: a whole 4x4x8 slice. The times are simulated.
256 devices in a mesh: region: 32 (over y, z_lo, core), group: 8 (over x, z_hi).
Axes of the slice: x: 4, y: 4, z: 8 (z_hi: 2, z_lo: 4; z = z_hi * 4 + z_lo), core: 2. Of those that a mesh axis runs over, the one named last changes fastest.
Arguments:
- node_latents: bfloat16 [262144, 512], P(('region', 'group')), may hold values from -6 to 6
- edge_latents: bfloat16 [1048576, 512], P(('region', 'group')), may hold values from -6 to 6
- senders: int32 [1048576], P(('region', 'group')), may hold values from 0 to 2559, as said below
- receiver_tile: int32 [8192], P(('region', 'group')), may hold values from 0 to 7
- receiver_row: int32 [1048576], P(('region', 'group')), may hold values from 0 to 127
- edge_mask: int32 [1048576], P(('region', 'group')), may hold values from 0 to 1, as said below
- send_map: int32 [256, 2, 2], replicated, may hold values from 0 to 7, as said below
- w_edge: bfloat16 [512, 512], replicated, may hold values from -0.15625 to 0.15625
- w_send: bfloat16 [512, 512], replicated, may hold values from -0.15625 to 0.15625
- w_recv: bfloat16 [512, 512], replicated, may hold values from -0.15625 to 0.15625
- w_edge_out: bfloat16 [512, 512], replicated, may hold values from -0.25 to 0.25
- w_node: bfloat16 [512, 512], replicated, may hold values from -0.1875 to 0.1875
- w_node_agg: bfloat16 [512, 512], replicated, may hold values from -0.1875 to 0.1875
- w_node_out: bfloat16 [512, 512], replicated, may hold values from -0.25 to 0.25
Outputs:
- new_nodes: bfloat16 [262144, 512], P(('region', 'group'))
- new_edges: bfloat16 [1048576, 512], P(('region', 'group'))
Inputs may be any that keep to these rules, and one draw needn't show every extreme that they name: `senders`: rows 0 to 1023 of a sender table are the device's own nodes, then 2 * 128 rows from the lower region, 256 from the upper, then 1024 coarse rows. `send_map`: the 2 tiles of one device and one direction are distinct. `edge_mask`: on each device the live edges come first, at least half of its slots.
All inputs are finite; a program needn't handle non-finite values.
Results may differ from a plain program's by a relative error of at most 0.0054.
Values may be sent and summed in bfloat16 or wider, within the bound.
No kernel may reach another device: no remote copies, remote signals or barrier semaphores. Data moves between devices by JAX's collectives and lax.ppermute only.
A program may use at most 128 MiB of HBM per device.

v0:
```python
import jax
import jax.numpy as jnp
from jax import lax
from jax.sharding import PartitionSpec as P

TILE = 128
CT = 1


def from_behind(x, axis, by):
    devices = lax.axis_size(axis)
    return lax.ppermute(x, axis, [(i, (i + by) % devices) for i in range(devices)])


def layer_norm(values):
    centred = values - jnp.mean(values, axis=-1, keepdims=True)
    return centred * lax.rsqrt(jnp.mean(centred * centred, axis=-1, keepdims=True) + 1e-05)


def per_device(
    node_latents,
    edge_latents,
    senders,
    receiver_tile,
    receiver_row,
    edge_mask,
    send_map,
    w_edge,
    w_send,
    w_recv,
    w_edge_out,
    w_node,
    w_node_agg,
    w_node_out,
):
    feature_width = node_latents.shape[1]
    node_rows = node_latents.shape[0]
    tile_count = node_rows // TILE
    regions = lax.axis_size("region")
    groups = lax.axis_size("group")
    region_id = lax.axis_index("region")
    group_id = lax.axis_index("group")
    lower_id = (region_id - 1) % regions * groups + group_id
    upper_id = (region_id + 1) % regions * groups + group_id
    own_proj = jnp.dot(node_latents, w_send, preferred_element_type=jnp.float32).astype(
        jnp.bfloat16
    )
    receiver_proj = jnp.dot(node_latents, w_recv, preferred_element_type=jnp.float32).astype(
        jnp.bfloat16
    )
    lower_block = from_behind(node_latents, "region", 1)
    upper_block = from_behind(node_latents, "region", -1)
    from_lower = lower_block.reshape(tile_count, TILE, feature_width)[
        send_map[lower_id, 1]
    ].reshape(-1, feature_width)
    from_upper = upper_block.reshape(tile_count, TILE, feature_width)[
        send_map[upper_id, 0]
    ].reshape(-1, feature_width)
    coarse_panel = lax.all_gather(node_latents[: CT * TILE], "group", axis=0, tiled=True)
    remote = jnp.concatenate([from_lower, from_upper, coarse_panel], axis=0)
    remote_proj = jnp.dot(remote, w_send, preferred_element_type=jnp.float32).astype(jnp.bfloat16)
    sender_table = jnp.concatenate([own_proj, remote_proj], axis=0)
    edge_tiles = receiver_tile.shape[0]
    row_in_tile = receiver_row.reshape(edge_tiles, TILE)
    receivers = (receiver_tile[:, None] * TILE + row_in_tile).reshape(-1)
    pre_act = jnp.dot(edge_latents, w_edge, preferred_element_type=jnp.float32)
    pre_act = (
        pre_act
        + sender_table[senders].astype(jnp.float32)
        + receiver_proj[receivers].astype(jnp.float32)
    )
    hidden = jax.nn.silu(pre_act).astype(jnp.bfloat16)
    edge_out = jnp.dot(hidden, w_edge_out, preferred_element_type=jnp.float32)
    message = layer_norm(edge_out) * edge_mask.astype(jnp.float32)[:, None]
    new_edges = (edge_latents.astype(jnp.float32) + message).astype(jnp.bfloat16)
    message_low = message.astype(jnp.bfloat16).reshape(edge_tiles, TILE, feature_width)
    row_ids = jnp.arange(TILE, dtype=jnp.int32)
    tile_hot = (row_ids[None, :, None] == row_in_tile[:, None, :]).astype(jnp.bfloat16)
    tile_sums = jnp.einsum(
        "tre,ted->trd", tile_hot, message_low, preferred_element_type=jnp.float32
    )
    tile_ids = jnp.arange(tile_count, dtype=jnp.int32)
    tile_owner = (tile_ids[:, None] == receiver_tile[None, :]).astype(jnp.float32)
    aggregated = jnp.einsum("nt,trd->nrd", tile_owner, tile_sums, precision=lax.Precision.HIGHEST)
    aggregated = aggregated.reshape(node_rows, feature_width).astype(jnp.bfloat16)
    node_pre = jnp.dot(node_latents, w_node, preferred_element_type=jnp.float32) + jnp.dot(
        aggregated, w_node_agg, preferred_element_type=jnp.float32
    )
    node_hidden = jax.nn.silu(node_pre).astype(jnp.bfloat16)
    node_out = jnp.dot(node_hidden, w_node_out, preferred_element_type=jnp.float32)
    new_nodes = (node_latents.astype(jnp.float32) + layer_norm(node_out)).astype(jnp.bfloat16)
    return (new_nodes, new_edges)


def solution(mesh):
    return jax.shard_map(
        per_device,
        mesh=mesh,
        in_specs=(
            P(("region", "group"), None),
            P(("region", "group"), None),
            P(("region", "group")),
            P(("region", "group")),
            P(("region", "group")),
            P(("region", "group")),
            P(),
            P(),
            P(),
            P(),
            P(),
            P(),
            P(),
            P(),
        ),
        out_specs=(P(("region", "group"), None), P(("region", "group"), None)),
        check_vma=False,
    )
```

profile of v0, /device:TPU:2, one launch (start us, length us, event | category | flops | bytes accessed | tf_op | source)
XLA Modules:
  0.0 152.6 jit_solution(5586843884704570277)
XLA Ops:
  7.2 0.0 copy-start
  7.2 0.0 all-gather.2.cloned.1.call-start
  7.2 0.1 collective-permute-start
  7.3 6.6 %collective-permute-start.1 = (bf16[1024,512]{1,0:T(8,128)(2,1)}, bf16[1024,512]{1,0:T(8,128)(2,1)}, u32[]{:S(2)}, u32[]{:S(2)}) collective-permute-start(bf16[1024,512]{1,0:T(8,128)(2,1)} %param.14), channel_id=1, source_target_pairs={{0,248},{8,0},{16,8},{24,16},{32,24},{40,32},{48,40},{56,48},{64,5... | collective-permute-start | bytes 3145736 | tf_op jit(solution)/shard_map/ppermute | solution.py:12
  13.9 1.6 %slice.3 = bf16[128,512]{1,0:T(8,128)(2,1)} slice(bf16[1024,512]{1,0:T(8,128)(2,1)} %param.14), slice={[0:128], [0:512]} | slice | bytes 262144 | tf_op jit(solution)/shard_map/slice | solution.py:59
  15.5 0.0 all-gather.2.cloned.1.call-update
  15.5 0.7 broadcast_multiply_fusion.2
  16.2 0.8 fusion.17
  17.0 2.3 %copy.18 = bf16[1024,512]{0,1:T(8,128)(2,1)} copy(bf16[1024,512]{1,0:T(8,128)(2,1)} %param.14) | data formatting | bytes 2097152 | tf_op args[0]
  19.2 0.7 convert_element_type.54
  20.0 2.1 %convolution_convert_fusion.1 = bf16[1024,512]{1,0:T(8,128)(2,1)S(1)} fusion(bf16[1024,512]{1,0:T(8,128)(2,1)} %param.14, bf16[512,512]{1,0:T(8,128)(2,1)} %param.23), kind=kOutput, calls=%fused_computation.25 | convolution fusion | flops 537395200 | bytes 2621440 | tf_op jit(solution)/shard_map/dot_general | solution.py:48
  22.1 17.3 %gather_fusion.3 = bf16[4096,512]{1,0:T(8,128)(2,1)} fusion(bf16[1024,512]{1,0:T(8,128)(2,1)S(1)} %convolution_convert_fusion.1, s32[4096]{0:T(1024)S(1)} %fusion.17), kind=kCustom, calls=%fused_computation.3 | custom fusion | bytes 8404992 | tf_op jit(solution)/shard_map/gather | solution.py:70
  39.4 0.2 dynamic-slice_reduce_fusion.1
  39.7 2.7 %convolution_convert_fusion.2 = bf16[1024,512]{1,0:T(8,128)(2,1)} fusion(bf16[1024,512]{1,0:T(8,128)(2,1)S(1)} %copy-done.2, bf16[512,512]{1,0:T(8,128)(2,1)} %param.22), kind=kOutput, calls=%fused_computation.26 | convolution fusion | flops 537395200 | bytes 2621440 | tf_op jit(solution)/shard_map/dot_general | solution.py:45
  42.4 2.0 %fusion.28 = f32[1024,512]{1,0:T(8,128)} fusion(bf16[1024,512]{1,0:T(8,128)(2,1)S(1)} %copy-done.2, bf16[512,512]{1,0:T(8,128)(2,1)S(1)} %copy-done.3), kind=kOutput, calls=%fused_computation.56 | convolution fusion | flops 536870912 | bytes 3670016 | tf_op jit(solution)/shard_map/dot_general | solution.py:86
  44.5 1.8 %gather_fusion = bf16[2,128,512]{2,1,0:T(8,128)(2,1)S(1)} fusion(bf16[8,128,512]{2,1,0:T(8,128)(2,1)} %bitcast.2, s32[1024]{0:T(1024)S(1)} %pad_clamp_fusion.1), kind=kCustom, calls=%fused_computation | custom fusion | bytes 524296 | tf_op jit(solution)/shard_map/gather | solution.py:53
  46.3 1.8 %gather_fusion.1 = bf16[2,128,512]{2,1,0:T(8,128)(2,1)S(1)} fusion(bf16[8,128,512]{2,1,0:T(8,128)(2,1)} %bitcast.5, s32[1024]{0:T(1024)S(1)} %pad_clamp_fusion), kind=kCustom, calls=%fused_computation.1 | custom fusion | bytes 524296 | tf_op jit(solution)/shard_map/gather | solution.py:56
  48.1 33.8 %all-gather.2.cloned.1.call-done = bf16[1024,512]{1,0:T(8,128)(2,1)} async-done(((bf16[128,512]{1,0:T(8,128)(2,1)}), bf16[1024,512]{1,0:T(8,128)(2,1)}) %all-gather.2.cloned.1.call-update) | async-done | bytes 1048592 | tf_op jit(solution)/shard_map/all_gather | solution.py:59
  81.9 2.2 %convolution_convert_fusion = bf16[1536,512]{1,0:T(8,128)(2,1)S(1)} fusion(bf16[512,512]{1,0:T(8,128)(2,1)S(1)} %copy-done.8, bf16[1024,512]{1,0:T(8,128)(2,1)} %all-gather.2.cloned.1.call-done, bf16[256,512]{1,0:T(8,128)(2,1)S(1)} %bitcast.39, bf16[256,512]{1,0:T(8,128)(2,1)S(1)} %bitcast.38), kind=kOutput, calls=%fused_computation.11 | convolution fusion | flops 810811392 | bytes 3670016 | tf_op jit(solution)/shard_map/dot_general | solution.py:61
  84.1 1.4 pad_maximum_fusion
  85.5 17.3 %gather_fusion.2 = bf16[4096,512]{1,0:T(8,128)(2,1)} fusion(bf16[2560,512]{1,0:T(8,128)(2,1)S(1)} %pad_maximum_fusion, s32[4096]{0:T(1024)S(1)} %fusion.16), kind=kCustom, calls=%fused_computation.2 | custom fusion | bytes 8404992 | tf_op jit(solution)/shard_map/gather | solution.py:69
  102.8 12.1 %fusion.26 = (f32[4096]{0:T(1024)S(1)}, f32[4096,512]{1,0:T(8,128)}) fusion(bf16[512,512]{1,0:T(8,128)(2,1)S(1)} %copy-done, bf16[4096,512]{1,0:T(8,128)(2,1)} %gather_fusion.3, bf16[4096,512]{1,0:T(8,128)(2,1)} %gather_fusion.2, bf16[4096,512]{1,0:T(8,128)(2,1)} %param.15, bf16[512,512]{1,0:T(8,128)(2,1)} %param.21), kind=kOutput, calls=%fused_computation.54 | convolution fusion | flops 4315934720 | bytes 22036480 | tf_op jit(solution)/shard_map/dot_general | solution.py:73
  114.9 4.4 %multiply_reduce_fusion = f32[4096]{0:T(1024)S(1)} fusion(f32[4096,512]{1,0:T(8,128)} %get-tuple-element.11, f32[4096]{0:T(1024)S(1)} %broadcast_multiply_fusion), kind=kLoop, calls=%fused_computation.8 | loop fusion | flops 6287360 | bytes 8421376 | tf_op jit(solution)/shard_map/reduce_sum | solution.py:17
  119.4 1.4 copy-done.1
  120.7 6.1 %add_convert_fusion = (bf16[4096,512]{1,0:T(8,128)(2,1)}, bf16[4096,512]{1,0:T(8,128)(2,1)S(1)}) fusion(bf16[4096,512]{1,0:T(8,128)(2,1)} %param.15, f32[4096,512]{1,0:T(8,128)S(1)} %copy-done.1, f32[4096]{0:T(1024)S(1)} %convert_element_type.54, f32[4096]{0:T(1024)S(1)} %add_rsqrt_fusion, f32[4096]{0:T(1024)S(1)} %broadcast_multiply_fusion), kind=kLoop, calls=%fused_computation.6 | loop fusion | flops 14680064 | bytes 21020672 | tf_op jit(solution)/shard_map/convert_element_type | solution.py:75
  126.8 1.2 fusion.3
  128.1 7.5 %fusion.10 = bf16[8,128,512]{2,0,1:T(8,128)(2,1)S(1)} fusion(f32[32,128,512]{2,1,0:T(8,128)S(1)} %fusion.3, s32[32]{0:T(128)S(1)} %copy-done.7), kind=kOutput, calls=%fused_computation.24 | convolution fusion | flops 201851136 | bytes 9437312 | tf_op jit(solution)/shard_map/nt,trd->nrd/dot_general | solution.py:84
  135.7 1.3 copy.19
  136.9 3.6 %fusion.27 = (f32[1024]{0:T(1024)S(1)}, f32[1024,512]{0,1:T(8,128)S(1)}) fusion(bf16[512,512]{1,0:T(8,128)(2,1)S(1)} %copy-done.9, f32[1024,512]{1,0:T(8,128)} %fusion.28, bf16[1024,512]{1,0:T(8,128)(2,1)} %bitcast.37, bf16[512,512]{1,0:T(8,128)(2,1)} %param.26), kind=kOutput, calls=%fused_computation.55 | convolution fusion | flops 1077410816 | bytes 6295552 | tf_op jit(solution)/shard_map/dot_general | solution.py:90
  140.6 0.3 multiply_reduce_fusion.1
  140.9 2.6 %add_convert_fusion.1 = bf16[1024,512]{0,1:T(8,128)(2,1)} fusion(bf16[1024,512]{0,1:T(8,128)(2,1)} %copy.18, f32[1024,512]{0,1:T(8,128)S(1)} %get-tuple-element.13, f32[1024]{0:T(1024)S(1)} %add_rsqrt_fusion.1, f32[1024]{0:T(1024)S(1)} %broadcast_multiply_fusion.1), kind=kLoop, calls=%fused_computation.13 | loop fusion | flops 2621440 | bytes 4202496 | tf_op jit(solution)/shard_map/convert_element_type | solution.py:91
  143.5 2.3 %copy.20 = bf16[1024,512]{1,0:T(8,128)(2,1)} copy(bf16[1024,512]{0,1:T(8,128)(2,1)} %add_convert_fusion.1) | data formatting | bytes 2097152
  (29 shorter events, 0.1 us)
Async XLA Ops:
  7.2 95.7 %copy-start = (bf16[512,512]{1,0:T(8,128)(2,1)S(1)}, bf16[512,512]{1,0:T(8,128)(2,1)}, u32[]{:S(2)}) copy-start(bf16[512,512]{1,0:T(8,128)(2,1)} %param.24) | copy-start | bytes 1572868
  7.2 74.7 %all-gather.2.cloned.1.call-start = ((), (), s32[]{:S(2)}) async-start(), calls=%async_computation | async-start | bytes 1179648 | tf_op jit(solution)/shard_map/all_gather | solution.py:59
  7.2 37.3 %collective-permute-start = (bf16[1024,512]{1,0:T(8,128)(2,1)}, bf16[1024,512]{1,0:T(8,128)(2,1)}, u32[]{:S(2)}, u32[]{:S(2)}) collective-permute-start(bf16[1024,512]{1,0:T(8,128)(2,1)} %param.14), channel_id=1, source_target_pairs={{0,8},{8,16},{16,24},{24,32},{32,40},{40,48},{48,56},{56,64},{64,7... | collective-permute-start | bytes 3145736 | tf_op jit(solution)/shard_map/ppermute | solution.py:12
  7.3 39.0 %collective-permute-start.1 = (bf16[1024,512]{1,0:T(8,128)(2,1)}, bf16[1024,512]{1,0:T(8,128)(2,1)}, u32[]{:S(2)}, u32[]{:S(2)}) collective-permute-start(bf16[1024,512]{1,0:T(8,128)(2,1)} %param.14), channel_id=1, source_target_pairs={{0,248},{8,0},{16,8},{24,16},{32,24},{40,32},{48,40},{56,48},{64,5... | collective-permute-start | bytes 3145736 | tf_op jit(solution)/shard_map/ppermute | solution.py:12
  22.0 17.4 %copy-start.6 = (s32[256,2,2]{0,2,1:T(2,128)S(1)}, s32[256,2,2]{0,2,1:T(2,128)}, u32[]{:S(2)}) copy-start(s32[256,2,2]{0,2,1:T(2,128)} %param.20) | copy-start | bytes 12292
  22.0 17.6 %copy-start.5 = (s32[4096]{0:T(1024)S(1)}, s32[4096]{0:T(1024)}, u32[]{:S(2)}) copy-start(s32[4096]{0:T(1024)} %param.16) | copy-start | bytes 49156
  22.0 17.7 %copy-start.2 = (bf16[1024,512]{1,0:T(8,128)(2,1)S(1)}, bf16[1024,512]{1,0:T(8,128)(2,1)}, u32[]{:S(2)}) copy-start(bf16[1024,512]{1,0:T(8,128)(2,1)} %param.14) | copy-start | bytes 3145732
  22.1 20.4 %copy-start.3 = (bf16[512,512]{1,0:T(8,128)(2,1)S(1)}, bf16[512,512]{1,0:T(8,128)(2,1)}, u32[]{:S(2)}) copy-start(bf16[512,512]{1,0:T(8,128)(2,1)} %param.25) | copy-start | bytes 1572868
  39.4 42.5 %copy-start.8 = (bf16[512,512]{1,0:T(8,128)(2,1)S(1)}, bf16[512,512]{1,0:T(8,128)(2,1)}, u32[]{:S(2)}) copy-start(bf16[512,512]{1,0:T(8,128)(2,1)} %param.22) | copy-start | bytes 1572868
  114.9 5.8 %copy-start.1 = (f32[4096,512]{1,0:T(8,128)S(1)}, f32[4096,512]{1,0:T(8,128)}, u32[]{:S(2)}) copy-start(f32[4096,512]{1,0:T(8,128)} %get-tuple-element.11) | copy-start | bytes 25165828
  120.7 6.1 %copy-start.4 = (s32[4096]{0:T(1024)S(1)}, s32[4096]{0:T(1024)}, u32[]{:S(2)}) copy-start(s32[4096]{0:T(1024)} %param.18) | copy-start | bytes 49156
  126.8 1.2 copy-start.7
  128.1 8.9 %copy-start.9 = (bf16[512,512]{1,0:T(8,128)(2,1)S(1)}, bf16[512,512]{1,0:T(8,128)(2,1)}, u32[]{:S(2)}) copy-start(bf16[512,512]{1,0:T(8,128)(2,1)} %param.27) | copy-start | bytes 1572868
Sparse Core Ops, SparseCore 0:
  15.6 66.2 all-gather.1
where the time goes:
time: 153 us
  local copies, waits for them, and re-layouts  47.3 us (31%)
  waiting for transfers between devices  33.8 us (22%)
  matrix products  33.5 us (22%)
  other arithmetic  17 us (11%)
  between operations  14.2 us (9%)
  starting transfers between devices  6.71 us (4%)
    all_gather x1, waiting for transfers between devices, per_device(): lax.all_gather(node_latents[:CT * TILE], 'group', axis=0, tiled=True)  33.8 us
    gather x1, local copies, waits for them, and re-layouts, per_device(): receiver_proj[receivers].astype(jnp.float32)  17.3 us
    gather x1, local copies, waits for them, and re-layouts, per_device(): sender_table[senders].astype(jnp.float32)  17.3 us
    dot_general x1, matrix products, per_device(): edge_out = jnp.dot(hidden, w_edge_out, preferred_element_type=jnp.float32)  12.1 us
    dot_general x1, matrix products, per_device(): jnp.einsum('nt,trd->nrd', tile_owner, tile_sums, precision=lax.Precision....  7.55 us
    ppermute x2, starting transfers between devices, from_behind(): lax.ppermute(x, axis, [(i, (i + by) % devices) for i in range(devices)])  6.68 us
    convert_element_type x1, other arithmetic, per_device(): (edge_latents.astype(jnp.float32) + message).astype(jnp.bfloat16)  6.1 us
    unnamed x22, local copies, waits for them, and re-layouts  5.98 us
  transfers between devices with their start and end apart: 3, of which 1 were waited for; matrix products, arithmetic and copies ran while one was open for 22% of the time, Pallas kernels for 0%

commit v1 on v0

v1 whole, which is shorter than its diff:
```python
import functools

import jax
import jax.numpy as jnp
from jax import lax
from jax.experimental import pallas as pl
from jax.experimental.pallas import tpu as pltpu
from jax.sharding import PartitionSpec as P

TILE = 128
D = 512
NTILE = 8
ETILE = 32
NODES = NTILE * TILE
EDGES = ETILE * TILE
REMOTE = 1536
TABLE = NODES + REMOTE
LANES = 128
PIECES = D // LANES
BLOCK = 512
BF = jnp.bfloat16
F32 = jnp.float32

ANY = pl.BlockSpec(memory_space=pl.ANY)
SMEM = pl.BlockSpec(memory_space=pltpu.SMEM)
VMEM = pl.BlockSpec(memory_space=pltpu.VMEM)


def in_vmem(x):
    return pltpu.with_memory_space_constraint(x, pltpu.VMEM)


def in_hbm(x):
    return pltpu.with_memory_space_constraint(x, pltpu.HBM)


def whole(shape):
    return pl.BlockSpec(shape, lambda i: (0,) * len(shape))


def dot(a, b):
    return jnp.dot(a, b, preferred_element_type=F32)


def silu(x):
    return x * (0.5 + 0.5 * jnp.tanh(0.5 * x))


def normed(v):
    centred = v - jnp.sum(v, axis=-1, keepdims=True) * (1.0 / D)
    var = jnp.sum(centred * centred, axis=-1, keepdims=True) * (1.0 / D)
    return centred, lax.rsqrt(var + 1e-05)


def put_rows(table, first, value):
    for c in range(PIECES):
        table[pl.ds(first * PIECES + c, value.shape[0], stride=PIECES), :] = value[
            :, c * LANES : (c + 1) * LANES
        ]


def get_rows(table, first, rows):
    return jnp.concatenate(
        [table[pl.ds(first * PIECES + c, rows, stride=PIECES), :] for c in range(PIECES)], axis=-1
    )


def one_hot(row_of_edge):
    rows = lax.broadcasted_iota(jnp.int32, (TILE, TILE), 0)
    return (rows == row_of_edge).astype(BF)


def pick_kernel(send_map, nodes, coarse, lower, upper, map_s, map_sem, sems):
    me = lax.axis_index("region") * lax.axis_size("group") + lax.axis_index("group")
    get_map = pltpu.make_async_copy(send_map, map_s, map_sem)
    get_map.start()
    copies = [pltpu.make_async_copy(nodes.at[pl.ds(0, TILE)], coarse, sems.at[0])]
    copies[0].start()
    get_map.wait()
    for side, out in ((0, lower), (1, upper)):
        for j in range(2):
            tile = map_s[side, j, me]
            copies.append(
                pltpu.make_async_copy(
                    nodes.at[pl.ds(pl.multiple_of(tile * TILE, TILE), TILE)],
                    out.at[pl.ds(j * TILE, TILE)],
                    sems.at[1 + side * 2 + j],
                )
            )
            copies[-1].start()
    for copy in copies:
        copy.wait()


def pick(node_latents, send_map):
    by_side = jnp.transpose(send_map, (1, 2, 0))
    return pl.pallas_call(
        pick_kernel,
        out_shape=[jax.ShapeDtypeStruct((rows, D), BF) for rows in (TILE, 2 * TILE, 2 * TILE)],
        in_specs=[ANY, ANY],
        out_specs=[VMEM] * 3,
        scratch_shapes=[
            pltpu.SMEM(by_side.shape, jnp.int32),
            pltpu.SemaphoreType.DMA,
            pltpu.SemaphoreType.DMA((5,)),
        ],
        compiler_params=pltpu.CompilerParams(vmem_limit_bytes=16 << 20),
        name="pick",
    )(in_hbm(by_side), in_hbm(node_latents))


def early_kernel(
    recv_tile, recv_row, nodes_h, edges_b, we_h, ws_h, wr_h, wn_h, weo_h, wna_h, wno_h,
    pre, edges, table, node_pre, nodes, ws, weo, wna, wno,
    we, wr, wn, recv_proj, sems,
):
    i = pl.program_id(0)
    pairs = [
        (nodes_h, nodes), (ws_h, ws), (wr_h, wr), (wn_h, wn), (we_h, we),
        (weo_h, weo), (wna_h, wna), (wno_h, wno),
    ]
    copies = [pltpu.make_async_copy(a, b, sems.at[j]) for j, (a, b) in enumerate(pairs)]

    @pl.when(i == 0)
    def _():
        for copy in copies:
            copy.start()
        for copy in copies:
            copy.wait()
        for k in range(NODES // BLOCK):
            part = slice(BLOCK * k, BLOCK * (k + 1))
            x = nodes[part]
            put_rows(table, BLOCK * k, dot(x, ws[...]).astype(BF).astype(F32))
            recv_proj[part] = dot(x, wr[...]).astype(BF)
            node_pre[part] = dot(x, wn[...])

    x = edges_b[...]
    here = pl.ds(pl.multiple_of(i * BLOCK, BLOCK), BLOCK)
    edges[here, :] = x
    own = dot(x, we[...])
    received = []
    for t in range(BLOCK // TILE):
        tile = recv_tile[i * (BLOCK // TILE) + t]
        hot = one_hot(recv_row[pl.ds(i * (BLOCK // TILE) + t, 1), :])
        received.append(
            lax.dot_general(
                hot,
                recv_proj[pl.ds(pl.multiple_of(tile * TILE, TILE), TILE), :],
                (((0,), (0,)), ((), ())),
                preferred_element_type=F32,
            )
        )
    pre[here, :] = own + jnp.concatenate(received)


def early(recv_tile, recv_row, nodes, edges, w_edge, w_send, w_recv, w_node, w_edge_out, w_node_agg, w_node_out):
    weight = pltpu.VMEM((D, D), BF)
    return pl.pallas_call(
        early_kernel,
        grid=(EDGES // BLOCK,),
        out_shape=[
            pltpu.VMEM((EDGES, D), F32),
            pltpu.VMEM((EDGES, D), BF),
            pltpu.VMEM((TABLE * PIECES, LANES), F32),
            pltpu.VMEM((NODES, D), F32),
            pltpu.VMEM((NODES, D), BF),
            weight, weight, weight, weight,
        ],
        in_specs=[SMEM, whole((ETILE, TILE)), ANY, pl.BlockSpec((BLOCK, D), lambda i: (i, 0))] + [ANY] * 7,
        out_specs=[VMEM] * 9,
        scratch_shapes=[weight, weight, weight, pltpu.VMEM((NODES, D), BF), pltpu.SemaphoreType.DMA((8,))],
        compiler_params=pltpu.CompilerParams(vmem_limit_bytes=20 << 20),
        cost_estimate=pl.CostEstimate(flops=8 << 30, bytes_accessed=24 << 20, transcendentals=0),
        name="early",
    )(
        recv_tile, recv_row, in_hbm(nodes), in_hbm(edges),
        *[in_hbm(w) for w in (w_edge, w_send, w_recv, w_node, w_edge_out, w_node_agg, w_node_out)],
    )


def late_kernel(
    senders, recv_tile, recv_row, mask,
    low, up, p_z, p_x1, p_x3, p_x2, p_z1, p_z3, p_z2,
    pre, edges, table_in, node_pre, nodes, ws, weo, wna, wno,
    out_nodes, out_edges, table,
    remote, picked, total, live, sems,
):
    i = pl.program_id(0)
    tiles = BLOCK // TILE

    @pl.when(i == 0)
    def _():
        me = lax.axis_index("group")
        panel = [
            (p_z, me ^ 1), (p_x1, (me + 6) % 8), (p_x3, (me + 2) % 8), (p_x2, (me + 4) % 8),
            (p_z1, ((me + 6) % 8) ^ 1), (p_z3, ((me + 2) % 8) ^ 1), (p_z2, ((me + 4) % 8) ^ 1),
        ]
        copies = [
            pltpu.make_async_copy(low, remote.at[pl.ds(0, 2 * TILE)], sems.at[0]),
            pltpu.make_async_copy(up, remote.at[pl.ds(2 * TILE, 2 * TILE)], sems.at[1]),
        ]
        for j, (piece, member) in enumerate(panel):
            at = pl.multiple_of(4 * TILE + member * TILE, TILE)
            copies.append(pltpu.make_async_copy(piece, remote.at[pl.ds(at, TILE)], sems.at[2 + j]))
        for copy in copies:
            copy.start()
        remote[pl.ds(pl.multiple_of(4 * TILE + me * TILE, TILE), TILE), :] = nodes[0:TILE, :]
        total[...] = jnp.zeros_like(total)
        live[0] = jnp.sum(mask[...])
        for copy in copies:
            copy.wait()
        for k in range(REMOTE // BLOCK):
            proj = dot(remote[BLOCK * k : BLOCK * (k + 1)], ws[...])
            put_rows(table, NODES + BLOCK * k, proj.astype(BF).astype(F32))

    first = pl.multiple_of(i * BLOCK, BLOCK)
    for e in range(BLOCK):
        row = senders[first + e]
        picked[e * PIECES : (e + 1) * PIECES, :] = table[
            pl.ds(pl.multiple_of(row * PIECES, PIECES), PIECES), :
        ]
    hidden = silu(pre[pl.ds(first, BLOCK), :] + get_rows(picked, 0, BLOCK)).astype(BF)
    centred, scale = normed(dot(hidden, weo[...]))
    slot = lax.broadcasted_iota(jnp.int32, (BLOCK, 1), 0) + first
    message = centred * jnp.where(slot < live[0], scale, 0.0)
    out_edges[...] = (edges[pl.ds(first, BLOCK), :].astype(F32) + message).astype(BF)
    rounded = message.astype(BF)
    for t in range(tiles):
        hot = one_hot(recv_row[pl.ds(i * tiles + t, 1), :])
        total[recv_tile[i * tiles + t]] += dot(hot, rounded[t * TILE : (t + 1) * TILE])

    @pl.when(i == EDGES // BLOCK - 1)
    def _():
        per = BLOCK // TILE
        for k in range(NODES // BLOCK):
            part = slice(BLOCK * k, BLOCK * (k + 1))
            summed = total[per * k : per * (k + 1)].reshape(BLOCK, D).astype(BF)
            hidden_n = silu(node_pre[part] + dot(summed, wna[...])).astype(BF)
            centred_n, scale_n = normed(dot(hidden_n, wno[...]))
            out_nodes[part, :] = (nodes[part].astype(F32) + centred_n * scale_n).astype(BF)


def late(senders, recv_tile, recv_row, mask, pieces, kept):
    return pl.pallas_call(
        late_kernel,
        grid=(EDGES // BLOCK,),
        out_shape=[
            jax.ShapeDtypeStruct((NODES, D), BF),
            jax.ShapeDtypeStruct((EDGES, D), BF),
            pltpu.VMEM((TABLE * PIECES, LANES), F32),
        ],
        in_specs=[SMEM, SMEM, whole((ETILE, TILE)), whole((ETILE, TILE))] + [ANY] * 9 + [VMEM] * 9,
        out_specs=[whole((NODES, D)), pl.BlockSpec((BLOCK, D), lambda i: (i, 0)), VMEM],
        input_output_aliases={15: 2},
        scratch_shapes=[
            pltpu.VMEM((REMOTE, D), BF),
            pltpu.VMEM((BLOCK * PIECES, LANES), F32),
            pltpu.VMEM((NTILE, TILE, D), F32),
            pltpu.SMEM((1,), jnp.int32),
            pltpu.SemaphoreType.DMA((9,)),
        ],
        compiler_params=pltpu.CompilerParams(vmem_limit_bytes=28 << 20),
        cost_estimate=pl.CostEstimate(flops=8 << 30, bytes_accessed=16 << 20, transcendentals=0),
        name="late",
    )(senders, recv_tile, recv_row, mask, *[in_hbm(p) for p in pieces], *[in_vmem(k) for k in kept])[:2]


def moved(x, axis, by):
    size = lax.axis_size(axis)
    return lax.ppermute(x, axis, [(i, (i + by) % size) for i in range(size)])


def per_device(
    node_latents, edge_latents, senders, receiver_tile, receiver_row, edge_mask, send_map,
    w_edge, w_send, w_recv, w_edge_out, w_node, w_node_agg, w_node_out,
):
    coarse, to_lower, to_upper = pick(node_latents, send_map)
    p_z = lax.ppermute(coarse, "group", [(i, i ^ 1) for i in range(8)])
    p_x = [moved(coarse, "group", by) for by in (2, 6, 4)]
    from_lower = moved(to_upper, "region", 1)
    from_upper = moved(to_lower, "region", -1)
    p_xz = [moved(p_z, "group", by) for by in (2, 6, 4)]
    recv_row = receiver_row.reshape(ETILE, TILE)
    kept = early(
        receiver_tile, recv_row, node_latents, edge_latents,
        w_edge, w_send, w_recv, w_node, w_edge_out, w_node_agg, w_node_out,
    )
    return late(
        senders, receiver_tile, recv_row, edge_mask.reshape(ETILE, TILE),
        [from_lower, from_upper, p_z] + p_x + p_xz, kept,
    )


def solution(mesh):
    by_device = P(("region", "group"))
    rows = P(("region", "group"), None)
    return jax.shard_map(
        per_device,
        mesh=mesh,
        in_specs=(rows, rows) + (by_device,) * 4 + (P(),) * 8,
        out_specs=(rows, rows),
        check_vma=False,
    )
```

time: 153 us -> 56.7 us (0.37)
  local copies, waits for them, and re-layouts: 47.3 us -> 2.25 us
  waiting for transfers between devices: 33.8 us -> 0.02 us
  matrix products: 33.5 us -> 0 us
  Pallas kernels: 0 us -> 31.5 us
  other arithmetic: 17 us -> 0 us
  starting transfers between devices: 6.71 us -> 21.7 us
  between operations: 14.2 us -> 0.8 us
    gather x4 -> x0, local copies, waits for them, and re-layouts: 38.2 us -> none  [the longest x1 17.3 us: per_device(): receiver_proj[receivers].astype(jnp.float32)]
    all_gather x1 -> x0, waiting for transfers between devices: 33.8 us -> none  [per_device(): lax.all_gather(node_latents[:CT * TILE], 'group', axis=0, tiled=True)]
    dot_general x8 -> x0, matrix products: 33.5 us -> none  [the longest x1 12.1 us: per_device(): edge_out = jnp.dot(hidden, w_edge_out, preferred_element_type=jnp.float32)]
    pallas_call x0 -> x3, Pallas kernels: none -> 31.5 us  [the longest x1 18 us: late(): pl.pallas_call(late_kernel, grid=(EDGES // BLOCK,), out_shape=[jax.ShapeD...]
    ppermute x2 -> x9, starting transfers between devices: 6.68 us -> 21.7 us  [the longest x8 14.5 us: moved(): return lax.ppermute(x, axis, [(i, (i + by) % size) for i in range(size)])]
    convert_element_type x3 -> x0, other arithmetic: 9.4 us -> none  [the longest x1 6.1 us: per_device(): (edge_latents.astype(jnp.float32) + message).astype(jnp.bfloat16)]
    reduce_sum x2 -> x0, other arithmetic: 4.72 us -> none  [layer_norm(): jnp.mean(centred * centred, axis=-1, keepdims=True) + 1e-05]
    unnamed x22 -> x30, local copies, waits for them, and re-layouts: 5.98 us -> 2.25 us
  transfers between devices with their start and end apart: 3 -> 9, of which waited for: 1 -> 0; matrix products, arithmetic and copies ran while one was open for 22% -> 0% of each run, Pallas kernels for 0% -> 21%
where the time goes in v1:
time: 56.7 us; the launch traced here: 56.3 us
  Pallas kernels  31.5 us (56%)
  starting transfers between devices  21.7 us (38%)
  local copies, waits for them, and re-layouts  2.25 us (4%)
  between operations  0.8 us (1%)
    pallas_call x1, Pallas kernels, late(): pl.pallas_call(late_kernel, grid=(EDGES // BLOCK,), out_shape=[jax.ShapeD...  18 us
    ppermute x8, starting transfers between devices, moved(): return lax.ppermute(x, axis, [(i, (i + by) % size) for i in range(size)])  14.5 us
    pallas_call x1, Pallas kernels, early(): pl.pallas_call(early_kernel, grid=(EDGES // BLOCK,), out_shape=[pltpu.VME...  11.7 us
    ppermute x1, starting transfers between devices, per_device(): p_z = lax.ppermute(coarse, 'group', [(i, i ^ 1) for i in range(8)])  7.19 us
    unnamed x30, local copies, waits for them, and re-layouts  2.25 us
    pallas_call x1, Pallas kernels, pick(): pl.pallas_call(pick_kernel, out_shape=[jax.ShapeDtypeStruct((rows, D), BF...  1.89 us
  transfers between devices with their start and end apart: 9, of which 0 were waited for; matrix products, arithmetic and copies ran while one was open for 0% of the time, Pallas kernels for 21%

profile of v1, /device:TPU:2, one launch (start us, length us, event | category | flops | bytes accessed | tf_op | source)
XLA Modules:
  0.0 56.3 jit_solution(16596194701306165989)
XLA Ops:
  0.6 1.9 %pick.1 = (bf16[128,512]{1,0:T(8,128)(2,1)S(1)}, bf16[256,512]{1,0:T(8,128)(2,1)S(1)}, bf16[256,512]{1,0:T(8,128)(2,1)S(1)}) custom-call(s32[2,2,256]{2,1,0:T(2,128)} %bitcast.6, bf16[1024,512]{1,0:T(8,128)(2,1)} %nodes_h.1), custom_call_target="tpu_custom_call" | custom-call | tf_op jit(solution)/shard_map/pick/pallas_call | solution.py:97
  2.5 2.2 %collective-permute-start.5 = (bf16[128,512]{1,0:T(8,128)(2,1)S(1)}, bf16[128,512]{1,0:T(8,128)(2,1)S(1)}, u32[]{:S(2)}, u32[]{:S(2)}) collective-permute-start(bf16[128,512]{1,0:T(8,128)(2,1)S(1)} %get-tuple-element.18), channel_id=1, source_target_pairs={{0,4},{1,5},{2,6},{3,7},{4,0},{5,1},{6,2},{7,3},{8,12},{9,13},{10,... | collective-permute-start | bytes 393224 | tf_op jit(solution)/shard_map/ppermute | solution.py:270
  4.7 7.2 %collective-permute-start.2 = (bf16[128,512]{1,0:T(8,128)(2,1)S(1)}, bf16[128,512]{1,0:T(8,128)(2,1)S(1)}, u32[]{:S(2)}, u32[]{:S(2)}) collective-permute-start(bf16[128,512]{1,0:T(8,128)(2,1)S(1)} %get-tuple-element.18), channel_id=1, source_target_pairs={{0,1},{1,0},{2,3},{3,2},{4,5},{5,4},{6,7},{7,6},{8,9},{9,8},{10,11... | collective-permute-start | bytes 393224 | tf_op jit(solution)/shard_map/ppermute | solution.py:278
  11.9 1.4 %collective-permute-start.4 = (bf16[128,512]{1,0:T(8,128)(2,1)S(1)}, bf16[128,512]{1,0:T(8,128)(2,1)S(1)}, u32[]{:S(2)}, u32[]{:S(2)}) collective-permute-start(bf16[128,512]{1,0:T(8,128)(2,1)S(1)} %get-tuple-element.18), channel_id=1, source_target_pairs={{0,6},{1,7},{2,0},{3,1},{4,2},{5,3},{6,4},{7,5},{8,14},{9,15},{10,... | collective-permute-start | bytes 393224 | tf_op jit(solution)/shard_map/ppermute | solution.py:270
  13.4 0.6 %collective-permute-start.3 = (bf16[128,512]{1,0:T(8,128)(2,1)S(1)}, bf16[128,512]{1,0:T(8,128)(2,1)S(1)}, u32[]{:S(2)}, u32[]{:S(2)}) collective-permute-start(bf16[128,512]{1,0:T(8,128)(2,1)S(1)} %get-tuple-element.18), channel_id=1, source_target_pairs={{0,2},{1,3},{2,4},{3,5},{4,6},{5,7},{6,0},{7,1},{8,10},{9,11},{10,... | collective-permute-start | bytes 393224 | tf_op jit(solution)/shard_map/ppermute | solution.py:270
  14.0 0.0 collective-permute-start
  14.0 0.0 collective-permute-done.5.p_x2
  14.0 5.6 %collective-permute-start.1 = (bf16[256,512]{1,0:T(8,128)(2,1)S(1)}, bf16[256,512]{1,0:T(8,128)(2,1)S(1)}, u32[]{:S(2)}, u32[]{:S(2)}) collective-permute-start(bf16[256,512]{1,0:T(8,128)(2,1)S(1)} %get-tuple-element.17), channel_id=1, source_target_pairs={{0,248},{8,0},{16,8},{24,16},{32,24},{40,32},{48,40},{56,48},{64,5... | collective-permute-start | bytes 786440 | tf_op jit(solution)/shard_map/ppermute | solution.py:270
  19.6 0.0 collective-permute-done.2.p_z
  19.6 2.6 %collective-permute-start.8 = (bf16[128,512]{1,0:T(8,128)(2,1)S(1)}, bf16[128,512]{1,0:T(8,128)(2,1)S(1)}, u32[]{:S(2)}, u32[]{:S(2)}) collective-permute-start(bf16[128,512]{1,0:T(8,128)(2,1)S(1)} %collective-permute-done.2.p_z), channel_id=1, source_target_pairs={{0,4},{1,5},{2,6},{3,7},{4,0},{5,1},{6,2},{7,3},{8,12},{9,13},{10,... | collective-permute-start | bytes 393224 | tf_op jit(solution)/shard_map/ppermute | solution.py:270
  22.2 0.0 collective-permute-done.4.p_x3
  22.2 0.0 collective-permute-start.7
  22.3 0.0 collective-permute-done.3.p_x1
  22.3 2.0 %collective-permute-start.6 = (bf16[128,512]{1,0:T(8,128)(2,1)S(1)}, bf16[128,512]{1,0:T(8,128)(2,1)S(1)}, u32[]{:S(2)}, u32[]{:S(2)}) collective-permute-start(bf16[128,512]{1,0:T(8,128)(2,1)S(1)} %collective-permute-done.2.p_z), channel_id=1, source_target_pairs={{0,2},{1,3},{2,4},{3,5},{4,6},{5,7},{6,0},{7,1},{8,10},{9,11},{10,... | collective-permute-start | bytes 393224 | tf_op jit(solution)/shard_map/ppermute | solution.py:270
  24.3 0.7 %copy-done.1 = s32[4096]{0:T(1024)S(1)} copy-done((s32[4096]{0:T(1024)S(1)}, s32[4096]{0:T(1024)}, u32[]{:S(2)}) %copy-start.1) | copy-done | bytes 16408
  25.0 0.7 %copy-done.4 = s32[32]{0:T(128)S(1)} copy-done((s32[32]{0:T(128)S(1)}, s32[32]{0:T(128)}, u32[]{:S(2)}) %copy-start.4) | copy-done | bytes 152
  25.7 11.7 %early.1 = (f32[4096,512]{1,0:T(8,128)S(1)}, bf16[4096,512]{1,0:T(8,128)(2,1)S(1)}, f32[10240,128]{1,0:T(8,128)S(1)}, f32[1024,512]{1,0:T(8,128)S(1)}, bf16[1024...) custom-call(s32[32]{0:T(128)S(1)} %copy-done.4, ...), custom_call_target="tpu_custom_call" | custom-call | flops 8589934592 | bytes 25165824 | tf_op jit(solution)/shard_map/early/pallas_call | solution.py:158
  37.3 0.0 copy-done.8
  37.4 0.0 copy-done.9
  37.4 0.0 copy-done.10
  37.4 0.0 copy-done.11
  37.4 0.0 collective-permute-done.8.p_z2
  37.4 0.0 collective-permute-done.7.p_z3
  37.4 0.0 collective-permute-done.6.p_z1
  37.4 0.0 collective-permute-done.low
  37.5 0.0 collective-permute-done.1.up
  37.5 0.6 copy-done.12
  38.0 0.0 copy-done.13
  38.1 0.1 copy-done.14
  38.1 0.1 copy-done.6
  38.2 0.1 copy-done.7
  38.3 18.0 %late.1 = (bf16[1024,512]{1,0:T(8,128)(2,1)}, bf16[4096,512]{1,0:T(8,128)(2,1)}, f32[10240,128]{1,0:T(8,128)S(1)}) custom-call(s32[4096]{0:T(1024)S(1)} %copy-done, s32[32]{0:T(128)S(1)} %copy-done.5, s32[32,128]{1,0:T(8,128)S(1)} %bitcast.4, s32[32,128]{1,0:T(8,128)S(1)} %bitcast.5, bf16[256,512]{1,0:T(8,128)(2,1)} %copy-done.6, ...), custom_call_target="tpu_custom_call", output_to_operand_aliasing={{2}: (15, {})} | custom-call | flops 8589934592 | bytes 16777216 | tf_op jit(solution)/shard_map/late/pallas_call | solution.py:244
  (19 shorter events, 0.0 us)
Async XLA Ops:
  2.5 11.4 %collective-permute-start.5 = (bf16[128,512]{1,0:T(8,128)(2,1)S(1)}, bf16[128,512]{1,0:T(8,128)(2,1)S(1)}, u32[]{:S(2)}, u32[]{:S(2)}) collective-permute-start(bf16[128,512]{1,0:T(8,128)(2,1)S(1)} %get-tuple-element.18), channel_id=1, source_target_pairs={{0,4},{1,5},{2,6},{3,7},{4,0},{5,1},{6,2},{7,3},{8,12},{9,13},{10,... | collective-permute-start | bytes 393224 | tf_op jit(solution)/shard_map/ppermute | solution.py:270
  4.7 14.9 %collective-permute-start.2 = (bf16[128,512]{1,0:T(8,128)(2,1)S(1)}, bf16[128,512]{1,0:T(8,128)(2,1)S(1)}, u32[]{:S(2)}, u32[]{:S(2)}) collective-permute-start(bf16[128,512]{1,0:T(8,128)(2,1)S(1)} %get-tuple-element.18), channel_id=1, source_target_pairs={{0,1},{1,0},{2,3},{3,2},{4,5},{5,4},{6,7},{7,6},{8,9},{9,8},{10,11... | collective-permute-start | bytes 393224 | tf_op jit(solution)/shard_map/ppermute | solution.py:278
  11.9 10.3 %collective-permute-start.4 = (bf16[128,512]{1,0:T(8,128)(2,1)S(1)}, bf16[128,512]{1,0:T(8,128)(2,1)S(1)}, u32[]{:S(2)}, u32[]{:S(2)}) collective-permute-start(bf16[128,512]{1,0:T(8,128)(2,1)S(1)} %get-tuple-element.18), channel_id=1, source_target_pairs={{0,6},{1,7},{2,0},{3,1},{4,2},{5,3},{6,4},{7,5},{8,14},{9,15},{10,... | collective-permute-start | bytes 393224 | tf_op jit(solution)/shard_map/ppermute | solution.py:270
  13.4 8.9 %collective-permute-start.3 = (bf16[128,512]{1,0:T(8,128)(2,1)S(1)}, bf16[128,512]{1,0:T(8,128)(2,1)S(1)}, u32[]{:S(2)}, u32[]{:S(2)}) collective-permute-start(bf16[128,512]{1,0:T(8,128)(2,1)S(1)} %get-tuple-element.18), channel_id=1, source_target_pairs={{0,2},{1,3},{2,4},{3,5},{4,6},{5,7},{6,0},{7,1},{8,10},{9,11},{10,... | collective-permute-start | bytes 393224 | tf_op jit(solution)/shard_map/ppermute | solution.py:270
  14.0 23.5 %collective-permute-start = (bf16[256,512]{1,0:T(8,128)(2,1)S(1)}, bf16[256,512]{1,0:T(8,128)(2,1)S(1)}, u32[]{:S(2)}, u32[]{:S(2)}) collective-permute-start(bf16[256,512]{1,0:T(8,128)(2,1)S(1)} %get-tuple-element.16), channel_id=1, source_target_pairs={{0,8},{8,16},{16,24},{24,32},{32,40},{40,48},{48,56},{56,64},{64,7... | collective-permute-start | bytes 786440 | tf_op jit(solution)/shard_map/ppermute | solution.py:270
  14.0 23.4 %copy-start.8 = (bf16[128,512]{1,0:T(8,128)(2,1)}, bf16[128,512]{1,0:T(8,128)(2,1)S(1)}, u32[]{:S(2)}) copy-start(bf16[128,512]{1,0:T(8,128)(2,1)S(1)} %collective-permute-done.5.p_x2) | copy-start | bytes 393220
  14.0 23.5 %collective-permute-start.1 = (bf16[256,512]{1,0:T(8,128)(2,1)S(1)}, bf16[256,512]{1,0:T(8,128)(2,1)S(1)}, u32[]{:S(2)}, u32[]{:S(2)}) collective-permute-start(bf16[256,512]{1,0:T(8,128)(2,1)S(1)} %get-tuple-element.17), channel_id=1, source_target_pairs={{0,248},{8,0},{16,8},{24,16},{32,24},{40,32},{48,40},{56,48},{64,5... | collective-permute-start | bytes 786440 | tf_op jit(solution)/shard_map/ppermute | solution.py:270
  19.6 17.7 %copy-start.9 = (bf16[128,512]{1,0:T(8,128)(2,1)}, bf16[128,512]{1,0:T(8,128)(2,1)S(1)}, u32[]{:S(2)}) copy-start(bf16[128,512]{1,0:T(8,128)(2,1)S(1)} %collective-permute-done.2.p_z) | copy-start | bytes 393220
  19.6 17.8 %collective-permute-start.8 = (bf16[128,512]{1,0:T(8,128)(2,1)S(1)}, bf16[128,512]{1,0:T(8,128)(2,1)S(1)}, u32[]{:S(2)}, u32[]{:S(2)}) collective-permute-start(bf16[128,512]{1,0:T(8,128)(2,1)S(1)} %collective-permute-done.2.p_z), channel_id=1, source_target_pairs={{0,4},{1,5},{2,6},{3,7},{4,0},{5,1},{6,2},{7,3},{8,12},{9,13},{10,... | collective-permute-start | bytes 393224 | tf_op jit(solution)/shard_map/ppermute | solution.py:270
  22.2 15.1 %copy-start.10 = (bf16[128,512]{1,0:T(8,128)(2,1)}, bf16[128,512]{1,0:T(8,128)(2,1)S(1)}, u32[]{:S(2)}) copy-start(bf16[128,512]{1,0:T(8,128)(2,1)S(1)} %collective-permute-done.4.p_x3) | copy-start | bytes 393220
  22.2 15.2 %collective-permute-start.7 = (bf16[128,512]{1,0:T(8,128)(2,1)S(1)}, bf16[128,512]{1,0:T(8,128)(2,1)S(1)}, u32[]{:S(2)}, u32[]{:S(2)}) collective-permute-start(bf16[128,512]{1,0:T(8,128)(2,1)S(1)} %collective-permute-done.2.p_z), channel_id=1, source_target_pairs={{0,6},{1,7},{2,0},{3,1},{4,2},{5,3},{6,4},{7,5},{8,14},{9,15},{10,... | collective-permute-start | bytes 393224 | tf_op jit(solution)/shard_map/ppermute | solution.py:270
  22.3 15.1 %copy-start.11 = (bf16[128,512]{1,0:T(8,128)(2,1)}, bf16[128,512]{1,0:T(8,128)(2,1)S(1)}, u32[]{:S(2)}) copy-start(bf16[128,512]{1,0:T(8,128)(2,1)S(1)} %collective-permute-done.3.p_x1) | copy-start | bytes 393220
  22.3 15.2 %collective-permute-start.6 = (bf16[128,512]{1,0:T(8,128)(2,1)S(1)}, bf16[128,512]{1,0:T(8,128)(2,1)S(1)}, u32[]{:S(2)}, u32[]{:S(2)}) collective-permute-start(bf16[128,512]{1,0:T(8,128)(2,1)S(1)} %collective-permute-done.2.p_z), channel_id=1, source_target_pairs={{0,2},{1,3},{2,4},{3,5},{4,6},{5,7},{6,0},{7,1},{8,10},{9,11},{10,... | collective-permute-start | bytes 393224 | tf_op jit(solution)/shard_map/ppermute | solution.py:270
  24.3 0.7 %copy-start.1 = (s32[4096]{0:T(1024)S(1)}, s32[4096]{0:T(1024)}, u32[]{:S(2)}) copy-start(s32[4096]{0:T(1024)} %param.18) | copy-start | bytes 49156
  25.0 0.7 %copy-start.4 = (s32[32]{0:T(128)S(1)}, s32[32]{0:T(128)}, u32[]{:S(2)}) copy-start(s32[32]{0:T(128)} %recv_tile.3) | copy-start | bytes 388
  25.7 12.7 %copy-start = (s32[4096]{0:T(1024)S(1)}, s32[4096]{0:T(1024)}, u32[]{:S(2)}) copy-start(s32[4096]{0:T(1024)} %senders.1) | copy-start | bytes 49156
  25.7 12.7 %copy-start.2 = (s32[4096]{0:T(1024)S(1)}, s32[4096]{0:T(1024)}, u32[]{:S(2)}) copy-start(s32[4096]{0:T(1024)} %param.18) | copy-start | bytes 49156
  25.7 12.7 %copy-start.3 = (s32[4096]{0:T(1024)S(1)}, s32[4096]{0:T(1024)}, u32[]{:S(2)}) copy-start(s32[4096]{0:T(1024)} %param.19) | copy-start | bytes 49156
  25.7 12.7 %copy-start.5 = (s32[32]{0:T(128)S(1)}, s32[32]{0:T(128)}, u32[]{:S(2)}) copy-start(s32[32]{0:T(128)} %recv_tile.3) | copy-start | bytes 388
  37.4 0.7 %copy-start.12 = (bf16[128,512]{1,0:T(8,128)(2,1)}, bf16[128,512]{1,0:T(8,128)(2,1)S(1)}, u32[]{:S(2)}) copy-start(bf16[128,512]{1,0:T(8,128)(2,1)S(1)} %collective-permute-done.8.p_z2) | copy-start | bytes 393220
  37.4 0.7 %copy-start.13 = (bf16[128,512]{1,0:T(8,128)(2,1)}, bf16[128,512]{1,0:T(8,128)(2,1)S(1)}, u32[]{:S(2)}) copy-start(bf16[128,512]{1,0:T(8,128)(2,1)S(1)} %collective-permute-done.7.p_z3) | copy-start | bytes 393220
  37.4 0.7 %copy-start.14 = (bf16[128,512]{1,0:T(8,128)(2,1)}, bf16[128,512]{1,0:T(8,128)(2,1)S(1)}, u32[]{:S(2)}) copy-start(bf16[128,512]{1,0:T(8,128)(2,1)S(1)} %collective-permute-done.6.p_z1) | copy-start | bytes 393220
  37.5 0.8 %copy-start.6 = (bf16[256,512]{1,0:T(8,128)(2,1)}, bf16[256,512]{1,0:T(8,128)(2,1)S(1)}, u32[]{:S(2)}) copy-start(bf16[256,512]{1,0:T(8,128)(2,1)S(1)} %collective-permute-done.low) | copy-start | bytes 786436
  37.5 0.8 %copy-start.7 = (bf16[256,512]{1,0:T(8,128)(2,1)}, bf16[256,512]{1,0:T(8,128)(2,1)S(1)}, u32[]{:S(2)}) copy-start(bf16[256,512]{1,0:T(8,128)(2,1)S(1)} %collective-permute-done.1.up) | copy-start | bytes 786436

commit v2 on v1

v2 whole, which is shorter than its diff:
```python
import functools

import jax
import jax.numpy as jnp
from jax import lax
from jax.experimental import pallas as pl
from jax.experimental.pallas import tpu as pltpu
from jax.sharding import PartitionSpec as P

TILE = 128
D = 512
NTILE = 8
ETILE = 32
NODES = NTILE * TILE
EDGES = ETILE * TILE
REMOTE = 1536
TABLE = NODES + REMOTE
LANES = 128
PIECES = D // LANES
BLOCK = 512
BF = jnp.bfloat16
F32 = jnp.float32

ANY = pl.BlockSpec(memory_space=pl.ANY)
SMEM = pl.BlockSpec(memory_space=pltpu.SMEM)
VMEM = pl.BlockSpec(memory_space=pltpu.VMEM)


def in_vmem(x):
    return pltpu.with_memory_space_constraint(x, pltpu.VMEM)


def in_hbm(x):
    return pltpu.with_memory_space_constraint(x, pltpu.HBM)


def whole(shape):
    return pl.BlockSpec(shape, lambda i: (0,) * len(shape))


def dot(a, b):
    return jnp.dot(a, b, preferred_element_type=F32)


def normed(v):
    centred = v - jnp.sum(v, axis=-1, keepdims=True) * (1.0 / D)
    var = jnp.sum(centred * centred, axis=-1, keepdims=True) * (1.0 / D)
    return centred, lax.rsqrt(var + 1e-05)


def put_rows(table, first, value):
    for c in range(PIECES):
        table[pl.ds(first * PIECES + c, value.shape[0], stride=PIECES), :] = value[
            :, c * LANES : (c + 1) * LANES
        ]


def get_rows(table, first, rows):
    return jnp.concatenate(
        [table[pl.ds(first * PIECES + c, rows, stride=PIECES), :] for c in range(PIECES)], axis=-1
    )


def one_hot(row_of_edge):
    rows = lax.broadcasted_iota(jnp.int32, (TILE, TILE), 0)
    return (rows == row_of_edge).astype(BF)


def first_kernel(nodes, coarse):
    coarse[...] = nodes[...]


def first_tile(node_latents):
    block = pl.BlockSpec((TILE, D), lambda i: (0, 0))
    return pl.pallas_call(
        first_kernel,
        grid=(1,),
        out_shape=jax.ShapeDtypeStruct((TILE, D), BF),
        in_specs=[block],
        out_specs=block,
        compiler_params=pltpu.CompilerParams(vmem_limit_bytes=4 << 20),
        name="first_tile",
    )(in_hbm(node_latents))


def project_kernel(
    send_map, nodes_h, ws_h, wr_h, wn_h, we_h, weo_h, wna_h, wno_h,
    coarse, lower, upper, table, node_pre, nodes, recv_proj, ws, we, weo, wna, wno,
    wr, wn, map_s, map_sem, sems, out_sems,
):
    me = lax.axis_index("region") * lax.axis_size("group") + lax.axis_index("group")
    get_map = pltpu.make_async_copy(send_map, map_s, map_sem)
    get_map.start()
    pairs = [
        (nodes_h, nodes), (ws_h, ws), (wr_h, wr), (wn_h, wn), (we_h, we),
        (weo_h, weo), (wna_h, wna), (wno_h, wno),
    ]
    copies = [pltpu.make_async_copy(a, b, sems.at[j]) for j, (a, b) in enumerate(pairs)]
    for copy in copies:
        copy.start()
    get_map.wait()
    copies[0].wait()
    sent = [pltpu.make_async_copy(nodes.at[pl.ds(0, TILE)], coarse, out_sems.at[0])]
    for side, out in ((0, lower), (1, upper)):
        for j in range(2):
            tile = map_s[side, j, me]
            sent.append(
                pltpu.make_async_copy(
                    nodes.at[pl.ds(pl.multiple_of(tile * TILE, TILE), TILE)],
                    out.at[pl.ds(j * TILE, TILE)],
                    out_sems.at[1 + side * 2 + j],
                )
            )
    for copy in sent:
        copy.start()
    for copy in copies[1:4]:
        copy.wait()
    for k in range(NODES // BLOCK):
        part = slice(BLOCK * k, BLOCK * (k + 1))
        x = nodes[part]
        put_rows(table, BLOCK * k, 0.5 * dot(x, ws[...]).astype(BF).astype(F32))
        recv_proj[part] = dot(x, wr[...]).astype(BF)
        node_pre[part] = dot(x, wn[...])
    for copy in copies[4:] + sent:
        copy.wait()


def project(send_map, nodes, w_send, w_recv, w_node, w_edge, w_edge_out, w_node_agg, w_node_out):
    weight = pltpu.VMEM((D, D), BF)
    by_side = jnp.transpose(send_map, (1, 2, 0))
    return pl.pallas_call(
        project_kernel,
        out_shape=[
            jax.ShapeDtypeStruct((TILE, D), BF),
            jax.ShapeDtypeStruct((2 * TILE, D), BF),
            jax.ShapeDtypeStruct((2 * TILE, D), BF),
            pltpu.VMEM((NODES * PIECES, LANES), F32),
            pltpu.VMEM((NODES, D), F32),
            pltpu.VMEM((NODES, D), BF),
            pltpu.VMEM((NODES, D), BF),
            weight, weight, weight, weight, weight,
        ],
        in_specs=[ANY] * 9,
        out_specs=[ANY] * 3 + [VMEM] * 9,
        scratch_shapes=[
            weight,
            weight,
            pltpu.SMEM(by_side.shape, jnp.int32),
            pltpu.SemaphoreType.DMA,
            pltpu.SemaphoreType.DMA((8,)),
            pltpu.SemaphoreType.DMA((5,)),
        ],
        compiler_params=pltpu.CompilerParams(vmem_limit_bytes=16 << 20),
        cost_estimate=pl.CostEstimate(flops=4 << 30, bytes_accessed=12 << 20, transcendentals=0),
        name="project",
    )(*[in_hbm(v) for v in (by_side, nodes, w_send, w_recv, w_node, w_edge, w_edge_out, w_node_agg, w_node_out)])


def early_kernel(recv_tile, recv_row, senders, edges_h, recv_proj, we, pre, edges, table_at, sems):
    blocks = EDGES // BLOCK
    tiles = BLOCK // TILE

    def get(b):
        here = pl.ds(pl.multiple_of(b * BLOCK, BLOCK), BLOCK)
        return pltpu.make_async_copy(edges_h.at[here], edges.at[here], sems.at[b])

    for b in range(blocks):
        get(b).start()
    table_at[...] = senders[...] * PIECES

    def body(b, _):
        get(b).wait()
        here = pl.ds(pl.multiple_of(b * BLOCK, BLOCK), BLOCK)
        own = dot(edges[here, :], we[...])
        received = []
        for t in range(tiles):
            tile = recv_tile[b * tiles + t]
            hot = one_hot(recv_row[pl.ds(b * tiles + t, 1), :])
            received.append(
                lax.dot_general(
                    hot,
                    recv_proj[pl.ds(pl.multiple_of(tile * TILE, TILE), TILE), :],
                    (((0,), (0,)), ((), ())),
                    preferred_element_type=F32,
                )
            )
        pre[here, :] = 0.5 * (own + jnp.concatenate(received))
        return 0

    lax.fori_loop(0, blocks, body, 0)


def early(recv_tile, recv_row, senders, edges, recv_proj, we):
    return pl.pallas_call(
        early_kernel,
        out_shape=[
            pltpu.VMEM((EDGES, D), F32),
            pltpu.VMEM((EDGES, D), BF),
            jax.ShapeDtypeStruct((ETILE, TILE), jnp.int32),
        ],
        in_specs=[SMEM, VMEM, VMEM, ANY, VMEM, VMEM],
        out_specs=[VMEM] * 3,
        scratch_shapes=[pltpu.SemaphoreType.DMA((EDGES // BLOCK,))],
        compiler_params=pltpu.CompilerParams(vmem_limit_bytes=16 << 20),
        cost_estimate=pl.CostEstimate(flops=8 << 30, bytes_accessed=24 << 20, transcendentals=0),
        name="early",
    )(recv_tile, recv_row, senders, in_hbm(edges), in_vmem(recv_proj), in_vmem(we))


def late_kernel(
    table_at, recv_tile, recv_row, mask,
    low, up, p_z, p_x1, p_x3, p_x2,
    pre, edges_in, own_table, node_pre, nodes, ws, weo, wna, wno,
    out_nodes, out_edges, edges,
    table, remote, picked, total, new_nodes, own_sem, sems, out_sems,
):
    tiles = BLOCK // TILE
    blocks = EDGES // BLOCK
    me = lax.axis_index("group")
    panel = [(p_z, me ^ 1)]
    for pair, member in ((p_x1, (me + 6) % 8), (p_x3, (me + 2) % 8), (p_x2, (me + 4) % 8)):
        panel.append((pair.at[pl.ds(0, TILE)], member))
        panel.append((pair.at[pl.ds(TILE, TILE)], member ^ 1))
    copies = [
        pltpu.make_async_copy(low, remote.at[pl.ds(0, 2 * TILE)], sems.at[0]),
        pltpu.make_async_copy(up, remote.at[pl.ds(2 * TILE, 2 * TILE)], sems.at[1]),
    ]
    for j, (piece, member) in enumerate(panel):
        at = pl.multiple_of(4 * TILE + member * TILE, TILE)
        copies.append(pltpu.make_async_copy(piece, remote.at[pl.ds(at, TILE)], sems.at[2 + j]))
    for copy in copies:
        copy.start()
    own = pltpu.make_async_copy(own_table, table.at[pl.ds(0, NODES * PIECES)], own_sem)
    own.start()

    remote[pl.ds(pl.multiple_of(4 * TILE + me * TILE, TILE), TILE), :] = nodes[0:TILE, :]
    total[...] = jnp.zeros_like(total)
    live = jnp.sum(mask[...])
    for copy in copies:
        copy.wait()
    for k in range(REMOTE // BLOCK):
        proj = dot(remote[BLOCK * k : BLOCK * (k + 1)], ws[...])
        put_rows(table, NODES + BLOCK * k, 0.5 * proj.astype(BF).astype(F32))
    own.wait()

    def put_edges(b):
        here = pl.ds(pl.multiple_of(b * BLOCK, BLOCK), BLOCK)
        return pltpu.make_async_copy(edges.at[here], out_edges.at[here], out_sems.at[b])

    def body(b, _):
        first = pl.multiple_of(b * BLOCK, BLOCK)
        here = pl.ds(first, BLOCK)
        for e in range(BLOCK):
            picked[e * PIECES : (e + 1) * PIECES, :] = table[
                pl.ds(pl.multiple_of(table_at[first + e], PIECES), PIECES), :
            ]
        half = pre[here, :] + get_rows(picked, 0, BLOCK)
        hidden = (half + half * jnp.tanh(half)).astype(BF)
        centred, scale = normed(dot(hidden, weo[...]))
        slot = lax.broadcasted_iota(jnp.int32, (BLOCK, 1), 0) + first
        message = centred * jnp.where(slot < live, scale, 0.0)
        edges[here, :] = (edges[here, :].astype(F32) + message).astype(BF)
        put_edges(b).start()
        rounded = message.astype(BF)
        for t in range(tiles):
            hot = one_hot(recv_row[pl.ds(b * tiles + t, 1), :])
            total[recv_tile[b * tiles + t]] += dot(hot, rounded[t * TILE : (t + 1) * TILE])
        return 0

    lax.fori_loop(0, blocks, body, 0)
    sent = []
    for k in range(NODES // BLOCK):
        part = slice(BLOCK * k, BLOCK * (k + 1))
        summed = total[tiles * k : tiles * (k + 1)].reshape(BLOCK, D).astype(BF)
        half_n = 0.5 * (node_pre[part] + dot(summed, wna[...]))
        hidden_n = (half_n + half_n * jnp.tanh(half_n)).astype(BF)
        centred_n, scale_n = normed(dot(hidden_n, wno[...]))
        new_nodes[part] = (nodes[part].astype(F32) + centred_n * scale_n).astype(BF)
        for t in range(tiles):
            here = pl.ds(BLOCK * k + TILE * t, TILE)
            sent.append(
                pltpu.make_async_copy(
                    new_nodes.at[here], out_nodes.at[here], out_sems.at[blocks + tiles * k + t]
                )
            )
            sent[-1].start()
    for copy in sent:
        copy.wait()
    for b in range(blocks):
        put_edges(b).wait()


def late(table_at, recv_tile, recv_row, mask, pieces, kept):
    blocks = EDGES // BLOCK
    return pl.pallas_call(
        late_kernel,
        out_shape=[
            jax.ShapeDtypeStruct((NODES, D), BF),
            jax.ShapeDtypeStruct((EDGES, D), BF),
            pltpu.VMEM((EDGES, D), BF),
        ],
        in_specs=[SMEM, SMEM, VMEM, VMEM] + [ANY] * 6 + [VMEM] * 9,
        out_specs=[ANY, ANY, VMEM],
        input_output_aliases={11: 2},
        scratch_shapes=[
            pltpu.VMEM((TABLE * PIECES, LANES), F32),
            pltpu.VMEM((REMOTE, D), BF),
            pltpu.VMEM((BLOCK * PIECES, LANES), F32),
            pltpu.VMEM((NTILE, TILE, D), F32),
            pltpu.VMEM((NODES, D), BF),
            pltpu.SemaphoreType.DMA,
            pltpu.SemaphoreType.DMA((9,)),
            pltpu.SemaphoreType.DMA((blocks + NTILE,)),
        ],
        compiler_params=pltpu.CompilerParams(vmem_limit_bytes=28 << 20),
        cost_estimate=pl.CostEstimate(flops=8 << 30, bytes_accessed=16 << 20, transcendentals=0),
        name="late",
    )(table_at, recv_tile, recv_row, mask, *pieces, *[in_vmem(k) for k in kept])[:2]


def joined_kernel(a, b, out, sems):
    copies = [
        pltpu.make_async_copy(a, out.at[pl.ds(0, TILE)], sems.at[0]),
        pltpu.make_async_copy(b, out.at[pl.ds(TILE, TILE)], sems.at[1]),
    ]
    for copy in copies:
        copy.start()
    for copy in copies:
        copy.wait()


def joined(a, b):
    return pl.pallas_call(
        joined_kernel,
        out_shape=jax.ShapeDtypeStruct((2 * TILE, D), BF),
        in_specs=[ANY, ANY],
        out_specs=VMEM,
        scratch_shapes=[pltpu.SemaphoreType.DMA((2,))],
        compiler_params=pltpu.CompilerParams(vmem_limit_bytes=4 << 20),
        name="joined",
    )(a, b)


def moved(x, axis, by):
    size = lax.axis_size(axis)
    return lax.ppermute(x, axis, [(i, (i + by) % size) for i in range(size)])


def per_device(
    node_latents, edge_latents, senders, receiver_tile, receiver_row, edge_mask, send_map,
    w_edge, w_send, w_recv, w_edge_out, w_node, w_node_agg, w_node_out,
):
    p_z = lax.ppermute(first_tile(node_latents), "group", [(i, i ^ 1) for i in range(8)])
    coarse, to_lower, to_upper, table, node_pre, nodes, recv_proj, ws, we, weo, wna, wno = project(
        send_map, node_latents, w_send, w_recv, w_node, w_edge, w_edge_out, w_node_agg, w_node_out
    )
    both = joined(coarse, p_z)
    p_x = [moved(both, "group", by) for by in (2, 6, 4)]
    from_lower = moved(to_upper, "region", 1)
    from_upper = moved(to_lower, "region", -1)
    recv_row = receiver_row.reshape(ETILE, TILE)
    pre, edges, table_at = early(
        receiver_tile, recv_row, senders.reshape(ETILE, TILE), edge_latents, recv_proj, we
    )
    return late(
        table_at.reshape(EDGES), receiver_tile, recv_row, edge_mask.reshape(ETILE, TILE),
        [from_lower, from_upper, p_z] + p_x,
        [pre, edges, table, node_pre, nodes, ws, weo, wna, wno],
    )


def solution(mesh):
    by_device = P(("region", "group"))
    rows = P(("region", "group"), None)
    return jax.shard_map(
        per_device,
        mesh=mesh,
        in_specs=(rows, rows) + (by_device,) * 4 + (P(),) * 8,
        out_specs=(rows, rows),
        check_vma=False,
    )
```

time: 56.7 us -> 47.1 us (0.83)
  starting transfers between devices: 21.7 us -> 17.2 us
  Pallas kernels: 31.5 us -> 28.4 us
  local copies, waits for them, and re-layouts: 2.25 us -> 0.01 us
    ppermute x8 -> x5, starting transfers between devices: 14.5 us -> 9.96 us  [moved(): return lax.ppermute(x, axis, [(i, (i + by) % size) for i in range(size)])]
    pallas_call x3 -> x5, Pallas kernels: 31.5 us -> 28.4 us  [the longest x1 16.6 us: late(): pl.pallas_call(late_kernel, out_shape=[jax.ShapeDtypeStruct((NODES, D), B...]
    unnamed x30 -> x8, local copies, waits for them, and re-layouts: 2.25 us -> 0.01 us
  transfers between devices with their start and end apart: 9 -> 6, of which waited for: 0 -> 2; matrix products, arithmetic and copies ran while one was open for 0% -> 0% of each run, Pallas kernels for 21% -> 23%
where the time goes in v2:
time: 47.1 us; the launch traced here: 46.7 us
  Pallas kernels  28.4 us (60%)
  starting transfers between devices  17.2 us (37%)
  between operations  0.7 us (1%)
    pallas_call x1, Pallas kernels, late(): pl.pallas_call(late_kernel, out_shape=[jax.ShapeDtypeStruct((NODES, D), B...  16.6 us
    ppermute x5, starting transfers between devices, moved(): return lax.ppermute(x, axis, [(i, (i + by) % size) for i in range(size)])  9.96 us
    ppermute x1, starting transfers between devices, per_device(): lax.ppermute(first_tile(node_latents), 'group', [(i, i ^ 1) for i in rang...  7.28 us
    pallas_call x1, Pallas kernels, early(): pl.pallas_call(early_kernel, out_shape=[pltpu.VMEM((EDGES, D), F32), pltp...  6.44 us
    pallas_call x1, Pallas kernels, project(): pl.pallas_call(project_kernel, out_shape=[jax.ShapeDtypeStruct((TILE, D),...  4.1 us
  transfers between devices with their start and end apart: 6, of which 2 were waited for; matrix products, arithmetic and copies ran while one was open for 0% of the time, Pallas kernels for 23%

profile of v2, /device:TPU:2, one launch (start us, length us, event | category | flops | bytes accessed | tf_op | source)
XLA Modules:
  0.0 46.7 jit_solution(11871393703923521337)
XLA Ops:
  0.6 0.9 %first_tile.1 = bf16[128,512]{1,0:T(8,128)(2,1)S(1)} custom-call(bf16[1024,512]{1,0:T(8,128)(2,1)} %nodes.1), custom_call_target="tpu_custom_call" | custom-call | tf_op jit(solution)/shard_map/first_tile/pallas_call | solution.py:75
  1.5 7.3 %collective-permute-start.2 = (bf16[128,512]{1,0:T(8,128)(2,1)S(1)}, bf16[128,512]{1,0:T(8,128)(2,1)S(1)}, u32[]{:S(2)}, u32[]{:S(2)}) collective-permute-start(bf16[128,512]{1,0:T(8,128)(2,1)S(1)} %first_tile.1), channel_id=1, source_target_pairs={{0,1},{1,0},{2,3},{3,2},{4,5},{5,4},{6,7},{7,6},{8,9},{9,8},{10,11... | collective-permute-start | bytes 393224 | tf_op jit(solution)/shard_map/ppermute | solution.py:353
  8.8 0.0 copy-start
  8.8 0.0 copy-start.1
  8.8 0.0 copy-start.3
  8.8 4.1 %project.1 = (bf16[128,512]{1,0:T(8,128)(2,1)S(1)}, bf16[256,512]{1,0:T(8,128)(2,1)S(1)}, bf16[256,512]{1,0:T(8,128)(2,1)S(1)}, f32[4096,128]{1,0:T(8,128)S(1)},...) custom-call(s32[2,2,256]{2,1,0:T(2,128)} %bitcast.10, ...), custom_call_target="tpu_custom_call" | custom-call | flops 4294967296 | bytes 12582912 | tf_op jit(solution)/shard_map/project/pallas_call | solution.py:131
  12.9 0.1 collective-permute-start
  13.0 5.6 %collective-permute-start.1 = (bf16[256,512]{1,0:T(8,128)(2,1)S(1)}, bf16[256,512]{1,0:T(8,128)(2,1)S(1)}, u32[]{:S(2)}, u32[]{:S(2)}) collective-permute-start(bf16[256,512]{1,0:T(8,128)(2,1)S(1)} %get-tuple-element.23), channel_id=1, source_target_pairs={{0,248},{8,0},{16,8},{24,16},{32,24},{40,32},{48,40},{56,48},{64,5... | collective-permute-start | bytes 786440 | tf_op jit(solution)/shard_map/ppermute | solution.py:346
  18.7 0.0 collective-permute-done.2.b.p_z
  18.7 0.3 joined.1
  19.0 2.2 %collective-permute-start.5 = (bf16[256,512]{1,0:T(8,128)(2,1)S(1)}, bf16[256,512]{1,0:T(8,128)(2,1)S(1)}, u32[]{:S(2)}, u32[]{:S(2)}) collective-permute-start(bf16[256,512]{1,0:T(8,128)(2,1)S(1)} %joined.1), channel_id=1, source_target_pairs={{0,4},{1,5},{2,6},{3,7},{4,0},{5,1},{6,2},{7,3},{8,12},{9,13},{10,... | collective-permute-start | bytes 786440 | tf_op jit(solution)/shard_map/ppermute | solution.py:346
  21.2 1.4 %collective-permute-start.4 = (bf16[256,512]{1,0:T(8,128)(2,1)S(1)}, bf16[256,512]{1,0:T(8,128)(2,1)S(1)}, u32[]{:S(2)}, u32[]{:S(2)}) collective-permute-start(bf16[256,512]{1,0:T(8,128)(2,1)S(1)} %joined.1), channel_id=1, source_target_pairs={{0,6},{1,7},{2,0},{3,1},{4,2},{5,3},{6,4},{7,5},{8,14},{9,15},{10,... | collective-permute-start | bytes 786440 | tf_op jit(solution)/shard_map/ppermute | solution.py:346
  22.7 0.6 %collective-permute-start.3 = (bf16[256,512]{1,0:T(8,128)(2,1)S(1)}, bf16[256,512]{1,0:T(8,128)(2,1)S(1)}, u32[]{:S(2)}, u32[]{:S(2)}) collective-permute-start(bf16[256,512]{1,0:T(8,128)(2,1)S(1)} %joined.1), channel_id=1, source_target_pairs={{0,2},{1,3},{2,4},{3,5},{4,6},{5,7},{6,0},{7,1},{8,10},{9,11},{10,... | collective-permute-start | bytes 786440 | tf_op jit(solution)/shard_map/ppermute | solution.py:346
  23.3 0.0 copy-done
  23.3 0.0 copy-done.1
  23.3 0.0 copy-done.3
  23.3 0.0 copy-start.2
  23.3 6.4 %early.1 = (f32[4096,512]{1,0:T(8,128)S(1)}, bf16[4096,512]{1,0:T(8,128)(2,1)S(1)}, s32[32,128]{1,0:T(8,128)S(1)}) custom-call(s32[32]{0:T(128)S(1)} %copy-done.3, s32[32,128]{1,0:T(8,128)S(1)} %bitcast.6, s32[32,128]{1,0:T(8,128)S(1)} %bitcast.5, bf16[4096,512]{1,0:T(8,128)(2,1)} %edges_h.1, bf16[1024,512]{1,0:T(8,128)(2,1)S(1)} %get-tuple-element.19.recv_proj, ...), custom_call_target="tpu_custom_call" | custom-call | flops 8589934592 | bytes 25165824 | tf_op jit(solution)/shard_map/early/pallas_call | solution.py:194
  29.7 0.0 collective-permute-done.low
  29.7 0.0 collective-permute-done.1.up
  29.7 0.0 collective-permute-done.5.p_x2
  29.7 0.2 collective-permute-done.4.p_x3
  30.0 0.1 collective-permute-done.3.p_x1
  30.0 0.0 copy-done.2
  30.0 16.6 %late.1 = (bf16[1024,512]{1,0:T(8,128)(2,1)}, bf16[4096,512]{1,0:T(8,128)(2,1)}, bf16[4096,512]{1,0:T(8,128)(2,1)S(1)}) custom-call(s32[4096]{0:T(1024)S(1)} %bitcast.9, s32[32]{0:T(128)S(1)} %copy-done.3, s32[32,128]{1,0:T(8,128)S(1)} %bitcast.7, s32[32,128]{1,0:T(8,128)S(1)} %bitcast.8, ...), custom_call_target="tpu_custom_call", output_to_operand_aliasing={{2}: (11, {})} | custom-call | flops 8589934592 | bytes 16777216 | tf_op jit(solution)/shard_map/late/pallas_call | solution.py:295
Async XLA Ops:
  1.5 17.1 %collective-permute-start.2 = (bf16[128,512]{1,0:T(8,128)(2,1)S(1)}, bf16[128,512]{1,0:T(8,128)(2,1)S(1)}, u32[]{:S(2)}, u32[]{:S(2)}) collective-permute-start(bf16[128,512]{1,0:T(8,128)(2,1)S(1)} %first_tile.1), channel_id=1, source_target_pairs={{0,1},{1,0},{2,3},{3,2},{4,5},{5,4},{6,7},{7,6},{8,9},{9,8},{10,11... | collective-permute-start | bytes 393224 | tf_op jit(solution)/shard_map/ppermute | solution.py:353
  8.8 14.4 %copy-start = (s32[4096]{0:T(1024)S(1)}, s32[4096]{0:T(1024)}, u32[]{:S(2)}) copy-start(s32[4096]{0:T(1024)} %param.16) | copy-start | bytes 49156
  8.8 14.4 %copy-start.1 = (s32[4096]{0:T(1024)S(1)}, s32[4096]{0:T(1024)}, u32[]{:S(2)}) copy-start(s32[4096]{0:T(1024)} %param.18) | copy-start | bytes 49156
  8.8 14.4 %copy-start.3 = (s32[32]{0:T(128)S(1)}, s32[32]{0:T(128)}, u32[]{:S(2)}) copy-start(s32[32]{0:T(128)} %recv_tile.3) | copy-start | bytes 388
  12.9 16.8 %collective-permute-start = (bf16[256,512]{1,0:T(8,128)(2,1)S(1)}, bf16[256,512]{1,0:T(8,128)(2,1)S(1)}, u32[]{:S(2)}, u32[]{:S(2)}) collective-permute-start(bf16[256,512]{1,0:T(8,128)(2,1)S(1)} %get-tuple-element.22), channel_id=1, source_target_pairs={{0,8},{8,16},{16,24},{24,32},{32,40},{40,48},{48,56},{56,64},{64,7... | collective-permute-start | bytes 786440 | tf_op jit(solution)/shard_map/ppermute | solution.py:346
  13.0 16.7 %collective-permute-start.1 = (bf16[256,512]{1,0:T(8,128)(2,1)S(1)}, bf16[256,512]{1,0:T(8,128)(2,1)S(1)}, u32[]{:S(2)}, u32[]{:S(2)}) collective-permute-start(bf16[256,512]{1,0:T(8,128)(2,1)S(1)} %get-tuple-element.23), channel_id=1, source_target_pairs={{0,248},{8,0},{16,8},{24,16},{32,24},{40,32},{48,40},{56,48},{64,5... | collective-permute-start | bytes 786440 | tf_op jit(solution)/shard_map/ppermute | solution.py:346
  19.0 10.7 %collective-permute-start.5 = (bf16[256,512]{1,0:T(8,128)(2,1)S(1)}, bf16[256,512]{1,0:T(8,128)(2,1)S(1)}, u32[]{:S(2)}, u32[]{:S(2)}) collective-permute-start(bf16[256,512]{1,0:T(8,128)(2,1)S(1)} %joined.1), channel_id=1, source_target_pairs={{0,4},{1,5},{2,6},{3,7},{4,0},{5,1},{6,2},{7,3},{8,12},{9,13},{10,... | collective-permute-start | bytes 786440 | tf_op jit(solution)/shard_map/ppermute | solution.py:346
  21.2 8.7 %collective-permute-start.4 = (bf16[256,512]{1,0:T(8,128)(2,1)S(1)}, bf16[256,512]{1,0:T(8,128)(2,1)S(1)}, u32[]{:S(2)}, u32[]{:S(2)}) collective-permute-start(bf16[256,512]{1,0:T(8,128)(2,1)S(1)} %joined.1), channel_id=1, source_target_pairs={{0,6},{1,7},{2,0},{3,1},{4,2},{5,3},{6,4},{7,5},{8,14},{9,15},{10,... | collective-permute-start | bytes 786440 | tf_op jit(solution)/shard_map/ppermute | solution.py:346
  22.7 7.4 %collective-permute-start.3 = (bf16[256,512]{1,0:T(8,128)(2,1)S(1)}, bf16[256,512]{1,0:T(8,128)(2,1)S(1)}, u32[]{:S(2)}, u32[]{:S(2)}) collective-permute-start(bf16[256,512]{1,0:T(8,128)(2,1)S(1)} %joined.1), channel_id=1, source_target_pairs={{0,2},{1,3},{2,4},{3,5},{4,6},{5,7},{6,0},{7,1},{8,10},{9,11},{10,... | collective-permute-start | bytes 786440 | tf_op jit(solution)/shard_map/ppermute | solution.py:346
  23.3 6.8 %copy-start.2 = (s32[4096]{0:T(1024)S(1)}, s32[4096]{0:T(1024)}, u32[]{:S(2)}) copy-start(s32[4096]{0:T(1024)} %param.19) | copy-start | bytes 49156

commit v3 on v2

--- a/solution.py
+++ b/solution.py
@@ -85,7 +85,7 @@
 
 def project_kernel(
     send_map, nodes_h, ws_h, wr_h, wn_h, we_h, weo_h, wna_h, wno_h,
-    coarse, lower, upper, table, node_pre, nodes, recv_proj, ws, we, weo, wna, wno,
+    coarse, inside, across, table, node_pre, nodes, recv_proj, ws, we, weo, wna, wno,
     wr, wn, map_s, map_sem, sems, out_sems,
 ):
     me = lax.axis_index("region") * lax.axis_size("group") + lax.axis_index("group")
@@ -101,14 +101,15 @@
     get_map.wait()
     copies[0].wait()
     sent = [pltpu.make_async_copy(nodes.at[pl.ds(0, TILE)], coarse, out_sems.at[0])]
-    for side, out in ((0, lower), (1, upper)):
+    odd = lax.rem(lax.axis_index("region"), 2)
+    for k, (side, out) in enumerate(((1 - odd, inside), (odd, across))):
         for j in range(2):
             tile = map_s[side, j, me]
             sent.append(
                 pltpu.make_async_copy(
                     nodes.at[pl.ds(pl.multiple_of(tile * TILE, TILE), TILE)],
                     out.at[pl.ds(j * TILE, TILE)],
-                    out_sems.at[1 + side * 2 + j],
+                    out_sems.at[1 + k * 2 + j],
                 )
             )
     for copy in sent:
@@ -134,7 +135,7 @@
             jax.ShapeDtypeStruct((TILE, D), BF),
             jax.ShapeDtypeStruct((2 * TILE, D), BF),
             jax.ShapeDtypeStruct((2 * TILE, D), BF),
-            pltpu.VMEM((NODES * PIECES, LANES), F32),
+            pltpu.VMEM((TABLE * PIECES, LANES), F32),
             pltpu.VMEM((NODES, D), F32),
             pltpu.VMEM((NODES, D), BF),
             pltpu.VMEM((NODES, D), BF),
@@ -156,7 +157,7 @@
     )(*[in_hbm(v) for v in (by_side, nodes, w_send, w_recv, w_node, w_edge, w_edge_out, w_node_agg, w_node_out)])
 
 
-def early_kernel(recv_tile, recv_row, senders, edges_h, recv_proj, we, pre, edges, table_at, sems):
+def early_kernel(recv_tile, recv_row, senders, edges_h, recv_proj, we, pre, edges, table_at, total, sems):
     blocks = EDGES // BLOCK
     tiles = BLOCK // TILE
 
@@ -167,6 +168,7 @@
     for b in range(blocks):
         get(b).start()
     table_at[...] = senders[...] * PIECES
+    total[...] = jnp.zeros_like(total)
 
     def body(b, _):
         get(b).wait()
@@ -197,9 +199,10 @@
             pltpu.VMEM((EDGES, D), F32),
             pltpu.VMEM((EDGES, D), BF),
             jax.ShapeDtypeStruct((ETILE, TILE), jnp.int32),
+            pltpu.VMEM((NTILE, TILE, D), F32),
         ],
         in_specs=[SMEM, VMEM, VMEM, ANY, VMEM, VMEM],
-        out_specs=[VMEM] * 3,
+        out_specs=[VMEM] * 4,
         scratch_shapes=[pltpu.SemaphoreType.DMA((EDGES // BLOCK,))],
         compiler_params=pltpu.CompilerParams(vmem_limit_bytes=16 << 20),
         cost_estimate=pl.CostEstimate(flops=8 << 30, bytes_accessed=24 << 20, transcendentals=0),
@@ -209,65 +212,78 @@
 
 def late_kernel(
     table_at, recv_tile, recv_row, mask,
-    low, up, p_z, p_x1, p_x3, p_x2,
-    pre, edges_in, own_table, node_pre, nodes, ws, weo, wna, wno,
-    out_nodes, out_edges, edges,
-    table, remote, picked, total, new_nodes, own_sem, sems, out_sems,
+    inside, across, p_z, p_xa, p_xb, p_x2,
+    pre, edges_in, table_in, total_in, node_pre, nodes, ws, weo, wna, wno,
+    out_nodes, out_edges, edges, table, total,
+    remote, picked, new_nodes, sems, out_sems,
 ):
     tiles = BLOCK // TILE
     blocks = EDGES // BLOCK
     me = lax.axis_index("group")
     panel = [(p_z, me ^ 1)]
-    for pair, member in ((p_x1, (me + 6) % 8), (p_x3, (me + 2) % 8), (p_x2, (me + 4) % 8)):
+    side_x = jnp.where(lax.rem(lax.div(me, 2), 2) == 1, lax.rem(me + 2, 8), lax.rem(me + 6, 8))
+    for pair, member in ((p_xa, me ^ 2), (p_xb, side_x), (p_x2, me ^ 4)):
         panel.append((pair.at[pl.ds(0, TILE)], member))
         panel.append((pair.at[pl.ds(TILE, TILE)], member ^ 1))
+    odd = lax.rem(lax.axis_index("region"), 2)
+    half_at = 2 * TILE
     copies = [
-        pltpu.make_async_copy(low, remote.at[pl.ds(0, 2 * TILE)], sems.at[0]),
-        pltpu.make_async_copy(up, remote.at[pl.ds(2 * TILE, 2 * TILE)], sems.at[1]),
+        pltpu.make_async_copy(inside, remote.at[pl.ds(pl.multiple_of((1 - odd) * half_at, half_at), half_at)], sems.at[0]),
+        pltpu.make_async_copy(across, remote.at[pl.ds(pl.multiple_of(odd * half_at, half_at), half_at)], sems.at[1]),
     ]
     for j, (piece, member) in enumerate(panel):
         at = pl.multiple_of(4 * TILE + member * TILE, TILE)
         copies.append(pltpu.make_async_copy(piece, remote.at[pl.ds(at, TILE)], sems.at[2 + j]))
     for copy in copies:
         copy.start()
-    own = pltpu.make_async_copy(own_table, table.at[pl.ds(0, NODES * PIECES)], own_sem)
-    own.start()
 
     remote[pl.ds(pl.multiple_of(4 * TILE + me * TILE, TILE), TILE), :] = nodes[0:TILE, :]
-    total[...] = jnp.zeros_like(total)
     live = jnp.sum(mask[...])
     for copy in copies:
         copy.wait()
     for k in range(REMOTE // BLOCK):
         proj = dot(remote[BLOCK * k : BLOCK * (k + 1)], ws[...])
         put_rows(table, NODES + BLOCK * k, 0.5 * proj.astype(BF).astype(F32))
-    own.wait()
 
     def put_edges(b):
         here = pl.ds(pl.multiple_of(b * BLOCK, BLOCK), BLOCK)
         return pltpu.make_async_copy(edges.at[here], out_edges.at[here], out_sems.at[b])
 
-    def body(b, _):
+    def take(b, slot, start, stop):
+        first = pl.multiple_of(b * BLOCK, BLOCK)
+        for e in range(start, stop):
+            to = (slot * BLOCK + e) * PIECES
+            picked[to : to + PIECES, :] = table[pl.ds(pl.multiple_of(table_at[first + e], PIECES), PIECES), :]
+
+    def edge_block(b, slot, b_next):
         first = pl.multiple_of(b * BLOCK, BLOCK)
         here = pl.ds(first, BLOCK)
-        for e in range(BLOCK):
-            picked[e * PIECES : (e + 1) * PIECES, :] = table[
-                pl.ds(pl.multiple_of(table_at[first + e], PIECES), PIECES), :
-            ]
-        half = pre[here, :] + get_rows(picked, 0, BLOCK)
+        half = pre[here, :] + get_rows(picked, slot * BLOCK, BLOCK)
         hidden = (half + half * jnp.tanh(half)).astype(BF)
-        centred, scale = normed(dot(hidden, weo[...]))
-        slot = lax.broadcasted_iota(jnp.int32, (BLOCK, 1), 0) + first
-        message = centred * jnp.where(slot < live, scale, 0.0)
-        edges[here, :] = (edges[here, :].astype(F32) + message).astype(BF)
+        out = dot(hidden, weo[...])
+        parts = []
+        for p in range(0, BLOCK, 32):
+            take(b_next, 1 - slot, p, p + 32)
+            centred, scale = normed(out[p : p + 32])
+            slots = lax.broadcasted_iota(jnp.int32, (32, 1), 0) + (first + p)
+            message = centred * jnp.where(slots < live, scale, 0.0)
+            there = pl.ds(pl.multiple_of(first + p, 32), 32)
+            edges[there, :] = (edges[there, :].astype(F32) + message).astype(BF)
+            parts.append(message.astype(BF))
         put_edges(b).start()
-        rounded = message.astype(BF)
+        rounded = jnp.concatenate(parts)
         for t in range(tiles):
             hot = one_hot(recv_row[pl.ds(b * tiles + t, 1), :])
             total[recv_tile[b * tiles + t]] += dot(hot, rounded[t * TILE : (t + 1) * TILE])
+
+    take(0, 0, 0, BLOCK)
+
+    def body(j, _):
+        edge_block(2 * j, 0, 2 * j + 1)
+        edge_block(2 * j + 1, 1, jnp.minimum(2 * j + 2, blocks - 1))
         return 0
 
-    lax.fori_loop(0, blocks, body, 0)
+    lax.fori_loop(0, blocks // 2, body, 0)
     sent = []
     for k in range(NODES // BLOCK):
         part = slice(BLOCK * k, BLOCK * (k + 1))
@@ -298,17 +314,16 @@
             jax.ShapeDtypeStruct((NODES, D), BF),
             jax.ShapeDtypeStruct((EDGES, D), BF),
             pltpu.VMEM((EDGES, D), BF),
+            pltpu.VMEM((TABLE * PIECES, LANES), F32),
+            pltpu.VMEM((NTILE, TILE, D), F32),
         ],
-        in_specs=[SMEM, SMEM, VMEM, VMEM] + [ANY] * 6 + [VMEM] * 9,
-        out_specs=[ANY, ANY, VMEM],
-        input_output_aliases={11: 2},
+        in_specs=[SMEM, SMEM, VMEM, VMEM] + [ANY] * 6 + [VMEM] * 10,
+        out_specs=[ANY, ANY, VMEM, VMEM, VMEM],
+        input_output_aliases={11: 2, 12: 3, 13: 4},
         scratch_shapes=[
-            pltpu.VMEM((TABLE * PIECES, LANES), F32),
             pltpu.VMEM((REMOTE, D), BF),
-            pltpu.VMEM((BLOCK * PIECES, LANES), F32),
-            pltpu.VMEM((NTILE, TILE, D), F32),
+            pltpu.VMEM((2 * BLOCK * PIECES, LANES), F32),
             pltpu.VMEM((NODES, D), BF),
-            pltpu.SemaphoreType.DMA,
             pltpu.SemaphoreType.DMA((9,)),
             pltpu.SemaphoreType.DMA((blocks + NTILE,)),
         ],
@@ -341,31 +356,35 @@
     )(a, b)
 
 
-def moved(x, axis, by):
-    size = lax.axis_size(axis)
-    return lax.ppermute(x, axis, [(i, (i + by) % size) for i in range(size)])
+def swapped(x, axis, partner):
+    return lax.ppermute(x, axis, [(i, partner(i)) for i in range(lax.axis_size(axis))])
 
 
 def per_device(
     node_latents, edge_latents, senders, receiver_tile, receiver_row, edge_mask, send_map,
     w_edge, w_send, w_recv, w_edge_out, w_node, w_node_agg, w_node_out,
 ):
-    p_z = lax.ppermute(first_tile(node_latents), "group", [(i, i ^ 1) for i in range(8)])
-    coarse, to_lower, to_upper, table, node_pre, nodes, recv_proj, ws, we, weo, wna, wno = project(
+    regions = lax.axis_size("region")
+    p_z = swapped(first_tile(node_latents), "group", lambda i: i ^ 1)
+    coarse, to_inside, to_across, table, node_pre, nodes, recv_proj, ws, we, weo, wna, wno = project(
         send_map, node_latents, w_send, w_recv, w_node, w_edge, w_edge_out, w_node_agg, w_node_out
     )
+    inside = swapped(to_inside, "region", lambda i: i ^ 1)
+    across = swapped(to_across, "region", lambda i: (i + 1 if i % 2 else i - 1) % regions)
     both = joined(coarse, p_z)
-    p_x = [moved(both, "group", by) for by in (2, 6, 4)]
-    from_lower = moved(to_upper, "region", 1)
-    from_upper = moved(to_lower, "region", -1)
+    p_x = [
+        swapped(both, "group", lambda i: i ^ 2),
+        swapped(both, "group", lambda i: (i + 2 if i // 2 % 2 else i - 2) % 8),
+        swapped(both, "group", lambda i: i ^ 4),
+    ]
     recv_row = receiver_row.reshape(ETILE, TILE)
-    pre, edges, table_at = early(
+    pre, edges, table_at, total = early(
         receiver_tile, recv_row, senders.reshape(ETILE, TILE), edge_latents, recv_proj, we
     )
     return late(
         table_at.reshape(EDGES), receiver_tile, recv_row, edge_mask.reshape(ETILE, TILE),
-        [from_lower, from_upper, p_z] + p_x,
-        [pre, edges, table, node_pre, nodes, ws, weo, wna, wno],
+        [inside, across, p_z] + p_x,
+        [pre, edges, table, total, node_pre, nodes, ws, weo, wna, wno],
     )
 
 

time: 47.1 us -> 45.8 us (0.972)
  Pallas kernels: 28.4 us -> 27.2 us
  waiting for transfers between devices: 0.3 us -> 1 us
  starting transfers between devices: 17.2 us -> 16.6 us
    pallas_call x1, Pallas kernels: 16.6 us -> 15.4 us  [late(): pl.pallas_call(late_kernel, out_shape=[jax.ShapeDtypeStruct((NODES, D), B...]
    ppermute x6, waiting for transfers between devices: 0.3 us -> 1 us  [swapped(): lax.ppermute(x, axis, [(i, partner(i)) for i in range(lax.axis_size(axis))])]
    ppermute x6, starting transfers between devices: 17.2 us -> 16.6 us  [swapped(): lax.ppermute(x, axis, [(i, partner(i)) for i in range(lax.axis_size(axis))])]
  transfers between devices with their start and end apart: 6 -> 6, of which waited for: 2 -> 2; matrix products, arithmetic and copies ran while one was open for 0% -> 0% of each run, Pallas kernels for 23% -> 24%
where the time goes in v3:
time: 45.8 us; the launch traced here: 45.6 us
  Pallas kernels  27.2 us (59%)
  starting transfers between devices  16.6 us (36%)
  waiting for transfers between devices  1 us (2%)
  between operations  0.7 us (2%)
    ppermute x6, starting transfers between devices, swapped(): lax.ppermute(x, axis, [(i, partner(i)) for i in range(lax.axis_size(axis))])  16.6 us
    pallas_call x1, Pallas kernels, late(): pl.pallas_call(late_kernel, out_shape=[jax.ShapeDtypeStruct((NODES, D), B...  15.4 us
    pallas_call x1, Pallas kernels, early(): pl.pallas_call(early_kernel, out_shape=[pltpu.VMEM((EDGES, D), F32), pltp...  6.45 us
    pallas_call x1, Pallas kernels, project(): pl.pallas_call(project_kernel, out_shape=[jax.ShapeDtypeStruct((TILE, D),...  4.12 us
    ppermute x6, waiting for transfers between devices, swapped(): lax.ppermute(x, axis, [(i, partner(i)) for i in range(lax.axis_size(axis))])  1 us
  transfers between devices with their start and end apart: 6, of which 2 were waited for; matrix products, arithmetic and copies ran while one was open for 0% of the time, Pallas kernels for 24%

profile of v3, /device:TPU:2, one launch (start us, length us, event | category | flops | bytes accessed | tf_op | source)
XLA Modules:
  0.0 45.6 jit_solution(944600578901767312)
XLA Ops:
  0.6 0.9 %first_tile.1 = bf16[128,512]{1,0:T(8,128)(2,1)S(1)} custom-call(bf16[1024,512]{1,0:T(8,128)(2,1)} %nodes.1), custom_call_target="tpu_custom_call" | custom-call | tf_op jit(solution)/shard_map/first_tile/pallas_call | solution.py:75
  1.5 7.3 %collective-permute-start.2 = (bf16[128,512]{1,0:T(8,128)(2,1)S(1)}, bf16[128,512]{1,0:T(8,128)(2,1)S(1)}, u32[]{:S(2)}, u32[]{:S(2)}) collective-permute-start(bf16[128,512]{1,0:T(8,128)(2,1)S(1)} %first_tile.1), channel_id=1, source_target_pairs={{0,1},{1,0},{2,3},{3,2},{4,5},{5,4},{6,7},{7,6},{8,9},{9,8},{10,11... | collective-permute-start | bytes 393224 | tf_op jit(solution)/shard_map/ppermute | solution.py:360
  8.8 0.0 copy-start
  8.8 0.0 copy-start.1
  8.8 0.0 copy-start.3
  8.8 4.1 %project.1 = (bf16[128,512]{1,0:T(8,128)(2,1)S(1)}, bf16[256,512]{1,0:T(8,128)(2,1)S(1)}, bf16[256,512]{1,0:T(8,128)(2,1)S(1)}, f32[10240,128]{1,0:T(8,128)S(1)}...) custom-call(s32[2,2,256]{2,1,0:T(2,128)} %bitcast.10, ...), custom_call_target="tpu_custom_call" | custom-call | flops 4294967296 | bytes 12582912 | tf_op jit(solution)/shard_map/project/pallas_call | solution.py:132
  13.0 0.1 collective-permute-start
  13.1 4.5 %collective-permute-start.1 = (bf16[256,512]{1,0:T(8,128)(2,1)S(1)}, bf16[256,512]{1,0:T(8,128)(2,1)S(1)}, u32[]{:S(2)}, u32[]{:S(2)}) collective-permute-start(bf16[256,512]{1,0:T(8,128)(2,1)S(1)} %get-tuple-element.24), channel_id=1, source_target_pairs={{0,248},{8,16},{16,8},{24,32},{32,24},{40,48},{48,40},{56,64},{64,... | collective-permute-start | bytes 786440 | tf_op jit(solution)/shard_map/ppermute | solution.py:360
  17.5 0.0 collective-permute-done.2.b.p_z
  17.5 0.3 joined.1
  17.9 2.2 %collective-permute-start.5 = (bf16[256,512]{1,0:T(8,128)(2,1)S(1)}, bf16[256,512]{1,0:T(8,128)(2,1)S(1)}, u32[]{:S(2)}, u32[]{:S(2)}) collective-permute-start(bf16[256,512]{1,0:T(8,128)(2,1)S(1)} %joined.1), channel_id=1, source_target_pairs={{0,4},{1,5},{2,6},{3,7},{4,0},{5,1},{6,2},{7,3},{8,12},{9,13},{10,... | collective-permute-start | bytes 786440 | tf_op jit(solution)/shard_map/ppermute | solution.py:360
  20.1 0.0 collective-permute-start.4
  20.1 2.6 %collective-permute-start.3 = (bf16[256,512]{1,0:T(8,128)(2,1)S(1)}, bf16[256,512]{1,0:T(8,128)(2,1)S(1)}, u32[]{:S(2)}, u32[]{:S(2)}) collective-permute-start(bf16[256,512]{1,0:T(8,128)(2,1)S(1)} %joined.1), channel_id=1, source_target_pairs={{0,2},{1,3},{2,0},{3,1},{4,6},{5,7},{6,4},{7,5},{8,10},{9,11},{10,... | collective-permute-start | bytes 786440 | tf_op jit(solution)/shard_map/ppermute | solution.py:360
  22.7 0.0 copy-done
  22.7 0.0 copy-done.1
  22.7 0.0 copy-done.3
  22.7 0.0 copy-start.2
  22.7 6.4 %early.1 = (f32[4096,512]{1,0:T(8,128)S(1)}, bf16[4096,512]{1,0:T(8,128)(2,1)S(1)}, s32[32,128]{1,0:T(8,128)S(1)}, f32[8,128,512]{2,1,0:T(8,128)S(1)}) custom-call(s32[32]{0:T(128)S(1)} %copy-done.3, s32[32,128]{1,0:T(8,128)S(1)} %bitcast.6, s32[32,128]{1,0:T(8,128)S(1)} %bitcast.5, bf16[4096,512]{1,0:T(8,128)(2,1)} %edges_h.1, ...), custom_call_target="tpu_custom_call" | custom-call | flops 8589934592 | bytes 25165824 | tf_op jit(solution)/shard_map/early/pallas_call | solution.py:196
  29.1 0.0 collective-permute-done.inside
  29.1 0.0 collective-permute-done.1.across
  29.2 0.0 collective-permute-done.5.p_x2
  29.2 0.9 %collective-permute-done.4.p_xb = bf16[256,512]{1,0:T(8,128)(2,1)S(1)} collective-permute-done((bf16[256,512]{1,0:T(8,128)(2,1)S(1)}, bf16[256,512]{1,0:T(8,128)(2,1)S(1)}, u32[]{:S(2)}, u32[]{:S(2)}) %collective-permute-start.4) | collective-permute-done | bytes 262176 | tf_op jit(solution)/shard_map/ppermute | solution.py:360
  30.0 0.1 collective-permute-done.3.p_xa
  30.2 0.0 copy-done.2
  30.2 15.4 %late.1 = (bf16[1024,512]{1,0:T(8,128)(2,1)}, bf16[4096,512]{1,0:T(8,128)(2,1)}, bf16[4096,512]{1,0:T(8,128)(2,1)S(1)}, f32[10240,128]{1,0:T(8,128)S(1)}, f32[8,128,512]{2,1,0:T(8,128)S(1)}) custom-call(s32[4096]{0:T(1024)S(1)} %bitcast.9, s32[32]{0:T(128)S(1)} %copy-done.3, ...), custom_call_target="tpu_custom_call", output_to_operand_aliasing={{2}: (11, {}), {3}: (12, {}), {4}: (13, {})} | custom-call | flops 8589934592 | bytes 16777216 | tf_op jit(solution)/shard_map/late/pallas_call | solution.py:311
Async XLA Ops:
  1.5 16.0 %collective-permute-start.2 = (bf16[128,512]{1,0:T(8,128)(2,1)S(1)}, bf16[128,512]{1,0:T(8,128)(2,1)S(1)}, u32[]{:S(2)}, u32[]{:S(2)}) collective-permute-start(bf16[128,512]{1,0:T(8,128)(2,1)S(1)} %first_tile.1), channel_id=1, source_target_pairs={{0,1},{1,0},{2,3},{3,2},{4,5},{5,4},{6,7},{7,6},{8,9},{9,8},{10,11... | collective-permute-start | bytes 393224 | tf_op jit(solution)/shard_map/ppermute | solution.py:360
  8.8 13.8 %copy-start = (s32[4096]{0:T(1024)S(1)}, s32[4096]{0:T(1024)}, u32[]{:S(2)}) copy-start(s32[4096]{0:T(1024)} %param.16) | copy-start | bytes 49156
  8.8 13.8 %copy-start.1 = (s32[4096]{0:T(1024)S(1)}, s32[4096]{0:T(1024)}, u32[]{:S(2)}) copy-start(s32[4096]{0:T(1024)} %param.18) | copy-start | bytes 49156
  8.8 13.8 %copy-start.3 = (s32[32]{0:T(128)S(1)}, s32[32]{0:T(128)}, u32[]{:S(2)}) copy-start(s32[32]{0:T(128)} %recv_tile.3) | copy-start | bytes 388
  13.0 16.2 %collective-permute-start = (bf16[256,512]{1,0:T(8,128)(2,1)S(1)}, bf16[256,512]{1,0:T(8,128)(2,1)S(1)}, u32[]{:S(2)}, u32[]{:S(2)}) collective-permute-start(bf16[256,512]{1,0:T(8,128)(2,1)S(1)} %get-tuple-element.23), channel_id=1, source_target_pairs={{0,8},{8,0},{16,24},{24,16},{32,40},{40,32},{48,56},{56,48},{64,72... | collective-permute-start | bytes 786440 | tf_op jit(solution)/shard_map/ppermute | solution.py:360
  13.1 16.1 %collective-permute-start.1 = (bf16[256,512]{1,0:T(8,128)(2,1)S(1)}, bf16[256,512]{1,0:T(8,128)(2,1)S(1)}, u32[]{:S(2)}, u32[]{:S(2)}) collective-permute-start(bf16[256,512]{1,0:T(8,128)(2,1)S(1)} %get-tuple-element.24), channel_id=1, source_target_pairs={{0,248},{8,16},{16,8},{24,32},{32,24},{40,48},{48,40},{56,64},{64,... | collective-permute-start | bytes 786440 | tf_op jit(solution)/shard_map/ppermute | solution.py:360
  17.9 11.3 %collective-permute-start.5 = (bf16[256,512]{1,0:T(8,128)(2,1)S(1)}, bf16[256,512]{1,0:T(8,128)(2,1)S(1)}, u32[]{:S(2)}, u32[]{:S(2)}) collective-permute-start(bf16[256,512]{1,0:T(8,128)(2,1)S(1)} %joined.1), channel_id=1, source_target_pairs={{0,4},{1,5},{2,6},{3,7},{4,0},{5,1},{6,2},{7,3},{8,12},{9,13},{10,... | collective-permute-start | bytes 786440 | tf_op jit(solution)/shard_map/ppermute | solution.py:360
  20.1 9.9 %collective-permute-start.4 = (bf16[256,512]{1,0:T(8,128)(2,1)S(1)}, bf16[256,512]{1,0:T(8,128)(2,1)S(1)}, u32[]{:S(2)}, u32[]{:S(2)}) collective-permute-start(bf16[256,512]{1,0:T(8,128)(2,1)S(1)} %joined.1), channel_id=1, source_target_pairs={{0,6},{1,7},{2,4},{3,5},{4,2},{5,3},{6,0},{7,1},{8,14},{9,15},{10,... | collective-permute-start | bytes 786440 | tf_op jit(solution)/shard_map/ppermute | solution.py:360
  20.1 10.1 %collective-permute-start.3 = (bf16[256,512]{1,0:T(8,128)(2,1)S(1)}, bf16[256,512]{1,0:T(8,128)(2,1)S(1)}, u32[]{:S(2)}, u32[]{:S(2)}) collective-permute-start(bf16[256,512]{1,0:T(8,128)(2,1)S(1)} %joined.1), channel_id=1, source_target_pairs={{0,2},{1,3},{2,0},{3,1},{4,6},{5,7},{6,4},{7,5},{8,10},{9,11},{10,... | collective-permute-start | bytes 786440 | tf_op jit(solution)/shard_map/ppermute | solution.py:360
  22.7 7.5 %copy-start.2 = (s32[4096]{0:T(1024)S(1)}, s32[4096]{0:T(1024)}, u32[]{:S(2)}) copy-start(s32[4096]{0:T(1024)} %param.19) | copy-start | bytes 49156

commit v4 on v3

--- a/solution.py
+++ b/solution.py
@@ -42,8 +42,7 @@
     return jnp.dot(a, b, preferred_element_type=F32)
 
 
-def normed(v):
-    centred = v - jnp.sum(v, axis=-1, keepdims=True) * (1.0 / D)
+def normed(centred):
     var = jnp.sum(centred * centred, axis=-1, keepdims=True) * (1.0 / D)
     return centred, lax.rsqrt(var + 1e-05)
 
@@ -124,6 +123,9 @@
         node_pre[part] = dot(x, wn[...])
     for copy in copies[4:] + sent:
         copy.wait()
+    for weight in (weo, wno):
+        w = weight[...].astype(F32)
+        weight[...] = (w - jnp.sum(w, axis=-1, keepdims=True) * (1.0 / D)).astype(BF)
 
 
 def project(send_map, nodes, w_send, w_recv, w_node, w_edge, w_edge_out, w_node_agg, w_node_out):
@@ -333,10 +335,12 @@
     )(table_at, recv_tile, recv_row, mask, *pieces, *[in_vmem(k) for k in kept])[:2]
 
 
-def joined_kernel(a, b, out, sems):
+def joined_kernel(a, b, inside_in, across_in, out, inside, across, sems):
     copies = [
         pltpu.make_async_copy(a, out.at[pl.ds(0, TILE)], sems.at[0]),
         pltpu.make_async_copy(b, out.at[pl.ds(TILE, TILE)], sems.at[1]),
+        pltpu.make_async_copy(inside_in, inside, sems.at[2]),
+        pltpu.make_async_copy(across_in, across, sems.at[3]),
     ]
     for copy in copies:
         copy.start()
@@ -344,16 +348,16 @@
         copy.wait()
 
 
-def joined(a, b):
+def joined(a, b, inside, across):
     return pl.pallas_call(
         joined_kernel,
-        out_shape=jax.ShapeDtypeStruct((2 * TILE, D), BF),
-        in_specs=[ANY, ANY],
-        out_specs=VMEM,
-        scratch_shapes=[pltpu.SemaphoreType.DMA((2,))],
+        out_shape=[jax.ShapeDtypeStruct((2 * TILE, D), BF)] * 3,
+        in_specs=[ANY] * 4,
+        out_specs=[VMEM] * 3,
+        scratch_shapes=[pltpu.SemaphoreType.DMA((4,))],
         compiler_params=pltpu.CompilerParams(vmem_limit_bytes=4 << 20),
         name="joined",
-    )(a, b)
+    )(a, b, inside, across)
 
 
 def swapped(x, axis, partner):
@@ -369,9 +373,9 @@
     coarse, to_inside, to_across, table, node_pre, nodes, recv_proj, ws, we, weo, wna, wno = project(
         send_map, node_latents, w_send, w_recv, w_node, w_edge, w_edge_out, w_node_agg, w_node_out
     )
+    both, to_inside, to_across = joined(coarse, p_z, to_inside, to_across)
     inside = swapped(to_inside, "region", lambda i: i ^ 1)
     across = swapped(to_across, "region", lambda i: (i + 1 if i % 2 else i - 1) % regions)
-    both = joined(coarse, p_z)
     p_x = [
         swapped(both, "group", lambda i: i ^ 2),
         swapped(both, "group", lambda i: (i + 2 if i // 2 % 2 else i - 2) % 8),

time: 45.8 us -> 44.3 us (0.967)
  waiting for transfers between devices: 1 us -> 0.02 us
  Pallas kernels: 27.2 us -> 26.5 us
    pallas_call x1, Pallas kernels: 15.4 us -> 14.2 us  [late(): pl.pallas_call(late_kernel, out_shape=[jax.ShapeDtypeStruct((NODES, D), B...]
    ppermute x6, waiting for transfers between devices: 1 us -> 0.02 us  [swapped(): lax.ppermute(x, axis, [(i, partner(i)) for i in range(lax.axis_size(axis))])]
  transfers between devices with their start and end apart: 6 -> 6, of which waited for: 2 -> 0; matrix products, arithmetic and copies ran while one was open for 0% -> 0% of each run, Pallas kernels for 24% -> 25%
where the time goes in v4:
time: 44.3 us; the launch traced here: 44 us
  Pallas kernels  26.5 us (60%)
  starting transfers between devices  16.8 us (38%)
  between operations  0.72 us (2%)
    ppermute x6, starting transfers between devices, swapped(): lax.ppermute(x, axis, [(i, partner(i)) for i in range(lax.axis_size(axis))])  16.8 us
    pallas_call x1, Pallas kernels, late(): pl.pallas_call(late_kernel, out_shape=[jax.ShapeDtypeStruct((NODES, D), B...  14.2 us
    pallas_call x1, Pallas kernels, early(): pl.pallas_call(early_kernel, out_shape=[pltpu.VMEM((EDGES, D), F32), pltp...  6.44 us
    pallas_call x1, Pallas kernels, project(): pl.pallas_call(project_kernel, out_shape=[jax.ShapeDtypeStruct((TILE, D),...  4.45 us
    pallas_call x1, Pallas kernels, first_tile(): pl.pallas_call(first_kernel, grid=(1,), out_shape=jax.ShapeDtypeStruct((T...  0.92 us
  transfers between devices with their start and end apart: 6, of which 0 were waited for; matrix products, arithmetic and copies ran while one was open for 0% of the time, Pallas kernels for 25%

profile of v4, /device:TPU:2, one launch (start us, length us, event | category | flops | bytes accessed | tf_op | source)
XLA Modules:
  0.0 44.0 jit_solution(15782992830301380516)
XLA Ops:
  0.6 0.9 %first_tile.1 = bf16[128,512]{1,0:T(8,128)(2,1)S(1)} custom-call(bf16[1024,512]{1,0:T(8,128)(2,1)} %nodes.1), custom_call_target="tpu_custom_call" | custom-call | tf_op jit(solution)/shard_map/first_tile/pallas_call | solution.py:74
  1.5 7.3 %collective-permute-start = (bf16[128,512]{1,0:T(8,128)(2,1)S(1)}, bf16[128,512]{1,0:T(8,128)(2,1)S(1)}, u32[]{:S(2)}, u32[]{:S(2)}) collective-permute-start(bf16[128,512]{1,0:T(8,128)(2,1)S(1)} %first_tile.1), channel_id=1, source_target_pairs={{0,1},{1,0},{2,3},{3,2},{4,5},{5,4},{6,7},{7,6},{8,9},{9,8},{10,11... | collective-permute-start | bytes 393224 | tf_op jit(solution)/shard_map/ppermute | solution.py:364
  8.8 0.0 copy-start
  8.8 0.0 copy-start.1
  8.8 0.0 copy-start.3
  8.8 4.4 %project.1 = (bf16[128,512]{1,0:T(8,128)(2,1)S(1)}, bf16[256,512]{1,0:T(8,128)(2,1)S(1)}, bf16[256,512]{1,0:T(8,128)(2,1)S(1)}, f32[10240,128]{1,0:T(8,128)S(1)}...) custom-call(s32[2,2,256]{2,1,0:T(2,128)} %bitcast.10, ...), custom_call_target="tpu_custom_call" | custom-call | flops 4294967296 | bytes 12582912 | tf_op jit(solution)/shard_map/project/pallas_call | solution.py:134
  13.3 0.0 collective-permute-done.b.p_z
  13.3 0.4 joined.1
  13.7 2.2 %collective-permute-start.5 = (bf16[256,512]{1,0:T(8,128)(2,1)S(1)}, bf16[256,512]{1,0:T(8,128)(2,1)S(1)}, u32[]{:S(2)}, u32[]{:S(2)}) collective-permute-start(bf16[256,512]{1,0:T(8,128)(2,1)S(1)} %get-tuple-element.31), channel_id=1, source_target_pairs={{0,4},{1,5},{2,6},{3,7},{4,0},{5,1},{6,2},{7,3},{8,12},{9,13},{10,... | collective-permute-start | bytes 786440 | tf_op jit(solution)/shard_map/ppermute | solution.py:364
  15.9 0.0 collective-permute-start.4
  15.9 2.6 %collective-permute-start.3 = (bf16[256,512]{1,0:T(8,128)(2,1)S(1)}, bf16[256,512]{1,0:T(8,128)(2,1)S(1)}, u32[]{:S(2)}, u32[]{:S(2)}) collective-permute-start(bf16[256,512]{1,0:T(8,128)(2,1)S(1)} %get-tuple-element.31), channel_id=1, source_target_pairs={{0,2},{1,3},{2,0},{3,1},{4,6},{5,7},{6,4},{7,5},{8,10},{9,11},{10,... | collective-permute-start | bytes 786440 | tf_op jit(solution)/shard_map/ppermute | solution.py:364
  18.5 0.0 collective-permute-start.1
  18.5 4.7 %collective-permute-start.2 = (bf16[256,512]{1,0:T(8,128)(2,1)S(1)}, bf16[256,512]{1,0:T(8,128)(2,1)S(1)}, u32[]{:S(2)}, u32[]{:S(2)}) collective-permute-start(bf16[256,512]{1,0:T(8,128)(2,1)S(1)} %get-tuple-element.30), channel_id=1, source_target_pairs={{0,248},{8,16},{16,8},{24,32},{32,24},{40,48},{48,40},{56,64},{64,... | collective-permute-start | bytes 786440 | tf_op jit(solution)/shard_map/ppermute | solution.py:364
  23.3 0.0 copy-done
  23.3 0.0 copy-done.1
  23.3 0.0 copy-done.3
  23.3 0.0 copy-start.2
  23.3 6.4 %early.1 = (f32[4096,512]{1,0:T(8,128)S(1)}, bf16[4096,512]{1,0:T(8,128)(2,1)S(1)}, s32[32,128]{1,0:T(8,128)S(1)}, f32[8,128,512]{2,1,0:T(8,128)S(1)}) custom-call(s32[32]{0:T(128)S(1)} %copy-done.3, s32[32,128]{1,0:T(8,128)S(1)} %bitcast.6, s32[32,128]{1,0:T(8,128)S(1)} %bitcast.5, bf16[4096,512]{1,0:T(8,128)(2,1)} %edges_h.1, ...), custom_call_target="tpu_custom_call" | custom-call | flops 8589934592 | bytes 25165824 | tf_op jit(solution)/shard_map/early/pallas_call | solution.py:198
  29.7 0.0 collective-permute-done.1.inside
  29.7 0.0 collective-permute-done.2.across
  29.7 0.0 collective-permute-done.5.p_x2
  29.8 0.0 collective-permute-done.4.p_xb
  29.8 0.0 collective-permute-done.3.p_xa
  29.8 0.0 copy-done.2
  29.8 14.2 %late.1 = (bf16[1024,512]{1,0:T(8,128)(2,1)}, bf16[4096,512]{1,0:T(8,128)(2,1)}, bf16[4096,512]{1,0:T(8,128)(2,1)S(1)}, f32[10240,128]{1,0:T(8,128)S(1)}, f32[8,128,512]{2,1,0:T(8,128)S(1)}) custom-call(s32[4096]{0:T(1024)S(1)} %bitcast.9, s32[32]{0:T(128)S(1)} %copy-done.3, ...), custom_call_target="tpu_custom_call", output_to_operand_aliasing={{2}: (11, {}), {3}: (12, {}), {4}: (13, {})} | custom-call | flops 8589934592 | bytes 16777216 | tf_op jit(solution)/shard_map/late/pallas_call | solution.py:313
Async XLA Ops:
  1.5 11.7 %collective-permute-start = (bf16[128,512]{1,0:T(8,128)(2,1)S(1)}, bf16[128,512]{1,0:T(8,128)(2,1)S(1)}, u32[]{:S(2)}, u32[]{:S(2)}) collective-permute-start(bf16[128,512]{1,0:T(8,128)(2,1)S(1)} %first_tile.1), channel_id=1, source_target_pairs={{0,1},{1,0},{2,3},{3,2},{4,5},{5,4},{6,7},{7,6},{8,9},{9,8},{10,11... | collective-permute-start | bytes 393224 | tf_op jit(solution)/shard_map/ppermute | solution.py:364
  8.8 14.4 %copy-start = (s32[4096]{0:T(1024)S(1)}, s32[4096]{0:T(1024)}, u32[]{:S(2)}) copy-start(s32[4096]{0:T(1024)} %param.16) | copy-start | bytes 49156
  8.8 14.4 %copy-start.1 = (s32[4096]{0:T(1024)S(1)}, s32[4096]{0:T(1024)}, u32[]{:S(2)}) copy-start(s32[4096]{0:T(1024)} %param.18) | copy-start | bytes 49156
  8.8 14.4 %copy-start.3 = (s32[32]{0:T(128)S(1)}, s32[32]{0:T(128)}, u32[]{:S(2)}) copy-start(s32[32]{0:T(128)} %recv_tile.3) | copy-start | bytes 388
  13.7 16.0 %collective-permute-start.5 = (bf16[256,512]{1,0:T(8,128)(2,1)S(1)}, bf16[256,512]{1,0:T(8,128)(2,1)S(1)}, u32[]{:S(2)}, u32[]{:S(2)}) collective-permute-start(bf16[256,512]{1,0:T(8,128)(2,1)S(1)} %get-tuple-element.31), channel_id=1, source_target_pairs={{0,4},{1,5},{2,6},{3,7},{4,0},{5,1},{6,2},{7,3},{8,12},{9,13},{10,... | collective-permute-start | bytes 786440 | tf_op jit(solution)/shard_map/ppermute | solution.py:364
  15.9 13.8 %collective-permute-start.4 = (bf16[256,512]{1,0:T(8,128)(2,1)S(1)}, bf16[256,512]{1,0:T(8,128)(2,1)S(1)}, u32[]{:S(2)}, u32[]{:S(2)}) collective-permute-start(bf16[256,512]{1,0:T(8,128)(2,1)S(1)} %get-tuple-element.31), channel_id=1, source_target_pairs={{0,6},{1,7},{2,4},{3,5},{4,2},{5,3},{6,0},{7,1},{8,14},{9,15},{10,... | collective-permute-start | bytes 786440 | tf_op jit(solution)/shard_map/ppermute | solution.py:364
  15.9 13.8 %collective-permute-start.3 = (bf16[256,512]{1,0:T(8,128)(2,1)S(1)}, bf16[256,512]{1,0:T(8,128)(2,1)S(1)}, u32[]{:S(2)}, u32[]{:S(2)}) collective-permute-start(bf16[256,512]{1,0:T(8,128)(2,1)S(1)} %get-tuple-element.31), channel_id=1, source_target_pairs={{0,2},{1,3},{2,0},{3,1},{4,6},{5,7},{6,4},{7,5},{8,10},{9,11},{10,... | collective-permute-start | bytes 786440 | tf_op jit(solution)/shard_map/ppermute | solution.py:364
  18.5 11.2 %collective-permute-start.1 = (bf16[256,512]{1,0:T(8,128)(2,1)S(1)}, bf16[256,512]{1,0:T(8,128)(2,1)S(1)}, u32[]{:S(2)}, u32[]{:S(2)}) collective-permute-start(bf16[256,512]{1,0:T(8,128)(2,1)S(1)} %get-tuple-element.29), channel_id=1, source_target_pairs={{0,8},{8,0},{16,24},{24,16},{32,40},{40,32},{48,56},{56,48},{64,72... | collective-permute-start | bytes 786440 | tf_op jit(solution)/shard_map/ppermute | solution.py:364
  18.5 11.2 %collective-permute-start.2 = (bf16[256,512]{1,0:T(8,128)(2,1)S(1)}, bf16[256,512]{1,0:T(8,128)(2,1)S(1)}, u32[]{:S(2)}, u32[]{:S(2)}) collective-permute-start(bf16[256,512]{1,0:T(8,128)(2,1)S(1)} %get-tuple-element.30), channel_id=1, source_target_pairs={{0,248},{8,16},{16,8},{24,32},{32,24},{40,48},{48,40},{56,64},{64,... | collective-permute-start | bytes 786440 | tf_op jit(solution)/shard_map/ppermute | solution.py:364
  23.3 6.5 %copy-start.2 = (s32[4096]{0:T(1024)S(1)}, s32[4096]{0:T(1024)}, u32[]{:S(2)}) copy-start(s32[4096]{0:T(1024)} %param.19) | copy-start | bytes 49156
